TPU v7x, 32 devices: a whole 2x2x4 slice. The times are simulated.
32 devices in a mesh: wide: 8 (over z, y), narrow: 4 (over x, core).
Axes of the slice: x: 2, y: 2, z: 4, core: 2. Of those that a mesh axis runs over, the one named last changes fastest.
Arguments:
- tokens: bfloat16 [16, 32, 32, 768], P('wide', 'narrow'), may hold values from -6 to 6
- cotangent: bfloat16 [16, 32, 32, 768], P('wide', 'narrow'), may hold values from -6 to 6
- conditioning: bfloat16 [8, 4608], P('wide'), may hold values from -4 to 4
- aspect: int32 [16, 2], replicated, may hold values from 16 to 32, as said below
- bucket: int32 [16], replicated, may hold values from 0 to 7, as said below
- qkv_weight: bfloat16 [768, 2304], replicated, may hold values from -0.21875 to 0.21875
- attn_kernel: bfloat16 [3, 3, 2304], replicated, may hold values from -2 to 2
- out_weight: bfloat16 [768, 768], replicated, may hold values from -2 to 2
- up_weight: bfloat16 [768, 3072], replicated, may hold values from -0.21875 to 0.21875
- ffn_kernel: bfloat16 [3, 3, 3072], replicated, may hold values from -2 to 2
- down_weight: bfloat16 [3072, 768], replicated, may hold values from -0.109375 to 0.109375
Outputs:
- block_out: bfloat16 [16, 32, 32, 768], P('wide', 'narrow')
- tokens_grad: bfloat16 [16, 32, 32, 768], P('wide', 'narrow')
- cond_grad: float32 [8, 3840], P('wide')
- shift_grad: float32 [8, 768], P('wide')
- qkv_grad: float32 [768, 2304], replicated
- attn_kernel_grad: float32 [3, 3, 2304], replicated
- out_grad: float32 [768, 768], replicated
- up_grad: float32 [768, 3072], replicated
- ffn_kernel_grad: float32 [3, 3, 3072], replicated
- down_grad: float32 [3072, 768], replicated
Inputs may be any that keep to these rules, and one draw needn't show every extreme that they name: In each aligned block of 2 items one item has aspect[i, 0] = 32; some item has a side of 16. bucket[i] is i // 2 or i // 2 + 1; the last 2 items have bucket 8 - 1; some bucket holds 4 items.
All inputs are finite; a program needn't handle non-finite values.
Results may differ from a plain program's by a relative error of at most 0.015.
The roundings to bfloat16 on the way count: a program that leaves them out, or rounds other values in their place, can miss the bound.
Values may be sent and summed in bfloat16 or wider, within the bound.
No kernel may reach another device: no remote copies, remote signals or barrier semaphores. Data moves between devices by JAX's collectives and lax.ppermute only.
A program may use at most 256 MiB of HBM per device.

v0:
```python
import jax
import jax.numpy as jnp
from jax import lax
from jax.sharding import PartitionSpec as P

HEAD_DIM = 64


masked_score = -1000000000.0
norm_epsilon = 1e-06


def extended(block, sides, width):
    for axis, dim in sides:
        count = lax.axis_size(axis)
        forward = [(i, i + 1) for i in range(count - 1)]
        backward = [(target, source) for source, target in forward]
        low = lax.ppermute(
            lax.slice_in_dim(block, block.shape[dim] - width, None, axis=dim), axis, forward
        )
        high = lax.ppermute(lax.slice_in_dim(block, 0, width, axis=dim), axis, backward)
        block = jnp.concatenate([low, block, high], axis=dim)
    return block


def from_behind(block, axis, distance):
    devices = range(lax.axis_size(axis))
    route = [(i - distance, i) for i in devices if i - distance in devices]
    return lax.ppermute(block, axis, route)


def modulate(values, shift, scale):
    center = values - jnp.mean(values, axis=-1, keepdims=True)
    spread_sq = jnp.mean(center * center, axis=-1, keepdims=True)
    return center * lax.rsqrt(spread_sq + norm_epsilon) * (1.0 + scale) + shift


def project(values, matrix):
    flat = values.reshape(-1, values.shape[-1])
    result = jnp.dot(flat, matrix, preferred_element_type=jnp.float32)
    return result.reshape(values.shape[:-1] + (matrix.shape[1],))


def project_back(grads, matrix):
    flat = grads.reshape(-1, grads.shape[-1])
    result = lax.dot_general(
        flat, matrix, (((1,), (1,)), ((), ())), preferred_element_type=jnp.float32
    )
    return result.reshape(grads.shape[:-1] + (matrix.shape[0],))


def weight_grad(left_side, right_side):
    left_flat = left_side.reshape(-1, left_side.shape[-1])
    right_flat = right_side.reshape(-1, right_side.shape[-1])
    return lax.dot_general(
        left_flat, right_flat, (((0,), (0,)), ((), ())), preferred_element_type=jnp.float32
    )


def pad_columns(values):
    return jnp.pad(values, ((0, 0), (0, 0), (1, 1), (0, 0)))


def margin_forward(values):
    return pad_columns(extended(values, (("narrow", 1),), 1))


def margin_backward(values):
    return pad_columns(extended(values, (("narrow", 1),), 1))


def spread(padded, kernel, row_count, col_count):
    total = jnp.zeros(padded.shape[:1] + (row_count, col_count) + padded.shape[3:], jnp.float32)
    for row_off in range(3):
        for col_off in range(3):
            total = (
                total
                + kernel[row_off, col_off]
                * padded[:, row_off : row_off + row_count, col_off : col_off + col_count]
            )
    return total


def spread_back(padded, kernel, row_count, col_count):
    total = jnp.zeros(padded.shape[:1] + (row_count, col_count) + padded.shape[3:], jnp.float32)
    for row_off in range(3):
        for col_off in range(3):
            total = (
                total
                + kernel[row_off, col_off]
                * padded[
                    :, 2 - row_off : 2 - row_off + row_count, 2 - col_off : 2 - col_off + col_count
                ]
            )
    return total


def kernel_grad(grads, padded, row_count, col_count):
    rows_out = []
    for row_off in range(3):
        cols_out = []
        for col_off in range(3):
            window = padded[:, row_off : row_off + row_count, col_off : col_off + col_count]
            cols_out.append(
                jnp.einsum("srcj,srcj->j", grads, window, preferred_element_type=jnp.float32)
            )
        rows_out.append(jnp.stack(cols_out, 0))
    return jnp.stack(rows_out, 0)


def to_phase(values):
    slot_count, row_count, col_count, chans = values.shape
    split = values.reshape(slot_count, row_count // 2, 2, col_count // 2, 2, chans).transpose(
        0, 2, 4, 1, 3, 5
    )
    split = split.reshape(slot_count, 4, row_count // 2, col_count // 2, chans)
    moved = lax.all_to_all(split, "narrow", split_axis=1, concat_axis=2, tiled=True)
    return moved.reshape(slot_count, -1, chans)


def to_rows(values, row_count, col_count):
    chans = values.shape[-1]
    half = col_count // 2
    slot_count = values.shape[0]
    split = values.reshape(slot_count, 1, half, half, chans)
    moved = lax.all_to_all(split, "narrow", split_axis=2, concat_axis=1, tiled=True)
    moved = moved.reshape(slot_count, 2, 2, row_count // 2, half, chans).transpose(0, 3, 1, 4, 2, 5)
    return moved.reshape(slot_count, row_count, col_count, chans)


def attention_scores(queries, keys_part, key_live):
    raw = jnp.einsum(
        "sqhd,skhd->shqk", queries, keys_part, preferred_element_type=jnp.float32
    ) * HEAD_DIM ** (-0.5)
    return jnp.where(key_live[:, None, None, :], raw, masked_score)


def on_device(
    tokens,
    cotangent,
    conditioning,
    aspect,
    bucket,
    qkv_weight,
    attn_kernel,
    out_weight,
    up_weight,
    ffn_kernel,
    down_weight,
):
    item_count = tokens.shape[0]
    row_count = tokens.shape[1]
    col_count = tokens.shape[2]
    width = tokens.shape[3]
    head_count = width // HEAD_DIM
    half = col_count // 2
    wide_at = lax.axis_index("wide")
    row_at = lax.axis_index("narrow")
    arrived = from_behind((tokens, cotangent), "wide", 1)
    inputs = jnp.concatenate([tokens, arrived[0]], 0)
    seeds = jnp.concatenate([cotangent, arrived[1]], 0)
    left_at = jnp.maximum(wide_at - 1, 0)
    own_bucket = lax.dynamic_slice_in_dim(bucket, wide_at * item_count, item_count)
    left_bucket = lax.dynamic_slice_in_dim(bucket, left_at * item_count, item_count)
    stays = own_bucket == wide_at
    alive = jnp.concatenate([stays, (left_bucket == wide_at) & (wide_at > 0)])
    sides = jnp.concatenate(
        [
            lax.dynamic_slice_in_dim(aspect, wide_at * item_count, item_count, 0),
            lax.dynamic_slice_in_dim(aspect, left_at * item_count, item_count, 0),
        ],
        0,
    )
    row_base = row_at * row_count
    local_slots = inputs.shape[0]
    local_rows = inputs.shape[1]
    heights = sides[:, 0]
    breadth = sides[:, 1]
    row_ids = row_base + jnp.arange(local_rows)
    col_ids = jnp.arange(col_count)
    token_mask = (
        (row_ids[None, :, None] < heights[:, None, None])
        & (col_ids[None, None, :] < breadth[:, None, None])
        & alive[:, None, None]
    ).astype(jnp.float32)
    factor = jnp.where(alive, col_count * col_count / (heights * breadth).astype(jnp.float32), 0.0)
    phase_rows = 2 * jnp.arange(half) + row_at // 2
    phase_cols = 2 * jnp.arange(half) + row_at % 2
    key_live = (
        (phase_rows[None, :, None] < heights[:, None, None])
        & (phase_cols[None, None, :] < breadth[:, None, None])
        & alive[:, None, None]
    ).reshape(local_slots, half * half)
    modul = conditioning[0].astype(jnp.float32)
    shift_one, scale_one, gate_one, shift_two, scale_two, gate_two = jnp.split(modul, 6)
    attn_k = attn_kernel.astype(jnp.float32)
    ffn_k = ffn_kernel.astype(jnp.float32)
    base = inputs.astype(jnp.float32) * token_mask[..., None]
    normed_one = modulate(base, shift_one, scale_one).astype(jnp.bfloat16)
    qkv = project(normed_one, qkv_weight).astype(jnp.bfloat16)
    qkv_padded = margin_forward(qkv)
    conv_qkv = spread(qkv_padded, attn_k, local_rows, col_count).astype(jnp.bfloat16)
    grouped = to_phase(conv_qkv)
    attn_slots = grouped.shape[0]
    group_len = grouped.shape[1]
    queries = grouped[:, :, :width].reshape(attn_slots, group_len, head_count, HEAD_DIM)
    keys_part = grouped[:, :, width : 2 * width].reshape(
        attn_slots, group_len, head_count, HEAD_DIM
    )
    value_part = grouped[:, :, 2 * width :].reshape(attn_slots, group_len, head_count, HEAD_DIM)
    scores = attention_scores(queries, keys_part, key_live)
    top_score = jnp.max(scores, axis=-1, keepdims=True)
    raised = jnp.exp(scores - top_score)
    totals = jnp.sum(raised, axis=-1, keepdims=True)
    probs = raised / totals
    log_total = top_score + jnp.log(totals)
    mixed = jnp.einsum(
        "shqk,skhd->sqhd",
        probs.astype(jnp.bfloat16),
        value_part,
        preferred_element_type=jnp.float32,
    )
    mixed = mixed.astype(jnp.bfloat16).reshape(attn_slots, group_len, width)
    mixed_grid = to_rows(mixed, local_rows, col_count)
    attended = project(mixed_grid, out_weight)
    middle = base + gate_one * attended
    normed_two = modulate(middle, shift_two, scale_two).astype(jnp.bfloat16)
    hidden = project(normed_two, up_weight).astype(jnp.bfloat16)
    hidden_padded = margin_forward(hidden)
    conv_hidden = spread(hidden_padded, ffn_k, local_rows, col_count)
    activated = jax.nn.gelu(conv_hidden).astype(jnp.bfloat16)
    branch = project(activated, down_weight)
    result = (token_mask[..., None] * (middle + gate_two * branch)).astype(jnp.bfloat16)
    seed = seeds.astype(jnp.float32) * factor[:, None, None, None]
    d_middle = token_mask[..., None] * seed
    d_gate_two = jnp.sum(d_middle * branch, axis=(0, 1, 2))
    d_branch = (d_middle * gate_two).astype(jnp.bfloat16)
    d_down = weight_grad(activated, d_branch)
    d_activated = project_back(d_branch, down_weight)
    gelu_value, gelu_back = jax.vjp(jax.nn.gelu, conv_hidden)
    d_conv_hidden = gelu_back(d_activated)[0].astype(jnp.bfloat16)
    d_hidden_padded = margin_backward(d_conv_hidden)
    d_hidden = spread_back(d_hidden_padded, ffn_k, local_rows, col_count).astype(jnp.bfloat16)
    d_ffn_kernel = kernel_grad(d_conv_hidden, hidden_padded, local_rows, col_count)
    d_up = weight_grad(normed_two, d_hidden)
    d_normed_two = project_back(d_hidden, up_weight)
    mod_value, mod_back_two = jax.vjp(modulate, middle, shift_two, scale_two)
    d_middle_more, d_shift_two, d_scale_two = mod_back_two(d_normed_two)
    d_middle = d_middle + d_middle_more
    d_gate_one = jnp.sum(d_middle * attended, axis=(0, 1, 2))
    d_attended = (d_middle * gate_one).astype(jnp.bfloat16)
    d_out = weight_grad(mixed_grid, d_attended)
    d_mixed_rows = project_back(d_attended, out_weight).astype(jnp.bfloat16)
    d_mixed = to_phase(d_mixed_rows).reshape(attn_slots, group_len, head_count, HEAD_DIM)
    again = attention_scores(queries, keys_part, key_live)
    probs_again = jnp.exp(again - log_total)
    d_value = jnp.einsum(
        "shqk,sqhd->skhd",
        probs_again.astype(jnp.bfloat16),
        d_mixed,
        preferred_element_type=jnp.float32,
    )
    d_probs = jnp.einsum("sqhd,skhd->shqk", d_mixed, value_part, preferred_element_type=jnp.float32)
    inner = jnp.sum(d_probs * probs_again, axis=-1, keepdims=True)
    d_scores = (probs_again * (d_probs - inner)).astype(jnp.bfloat16)
    d_queries = jnp.einsum(
        "shqk,skhd->sqhd", d_scores, keys_part, preferred_element_type=jnp.float32
    ) * HEAD_DIM ** (-0.5)
    d_keys = jnp.einsum(
        "shqk,sqhd->skhd", d_scores, queries, preferred_element_type=jnp.float32
    ) * HEAD_DIM ** (-0.5)
    d_grouped = jnp.concatenate(
        [
            d_queries.reshape(attn_slots, group_len, width),
            d_keys.reshape(attn_slots, group_len, width),
            d_value.reshape(attn_slots, group_len, width),
        ],
        -1,
    ).astype(jnp.bfloat16)
    d_conv_qkv = to_rows(d_grouped, local_rows, col_count)
    d_conv_padded = margin_backward(d_conv_qkv)
    d_qkv = spread_back(d_conv_padded, attn_k, local_rows, col_count).astype(jnp.bfloat16)
    d_attn_kernel = kernel_grad(d_conv_qkv, qkv_padded, local_rows, col_count)
    d_qkv_weight = weight_grad(normed_one, d_qkv)
    d_normed_one = project_back(d_qkv, qkv_weight)
    mod_first, mod_back_one = jax.vjp(modulate, base, shift_one, scale_one)
    d_base_more, d_shift_one, d_scale_one = mod_back_one(d_normed_one)
    d_base = d_middle + d_base_more
    input_grad = (token_mask[..., None] * d_base).astype(jnp.bfloat16)
    cond_part = jnp.concatenate([d_shift_one, d_scale_one, d_gate_one, d_scale_two, d_gate_two])[
        None, :
    ]
    shift_part = d_shift_two[None, :]
    cond_total, shift_total = lax.psum((cond_part, shift_part), "narrow")
    sent_back = from_behind((result[item_count:], input_grad[item_count:]), "wide", -1)
    keep = stays[:, None, None, None]
    block_out = jnp.where(keep, result[:item_count], sent_back[0])
    tokens_grad = jnp.where(keep, input_grad[:item_count], sent_back[1])
    grads = (d_qkv_weight, d_attn_kernel, d_out, d_up, d_ffn_kernel, d_down)
    flat = jnp.concatenate([g.reshape(-1) for g in grads])
    owned = lax.psum_scatter(flat, ("wide", "narrow"), scatter_dimension=0, tiled=True)
    summed = lax.all_gather(
        owned.astype(jnp.bfloat16), ("wide", "narrow"), axis=0, tiled=True
    ).astype(owned.dtype)
    pieces = []
    offset = 0
    for grad_part in grads:
        length = grad_part.size
        pieces.append(summed[offset : offset + length].reshape(grad_part.shape))
        offset = offset + length
    return (
        block_out,
        tokens_grad,
        cond_total,
        shift_total,
        pieces[0],
        pieces[1],
        pieces[2],
        pieces[3],
        pieces[4],
        pieces[5],
    )


def solution(mesh):
    in_specs = (
        P("wide", "narrow", None, None),
        P("wide", "narrow", None, None),
        P("wide", None),
        P(),
        P(),
        P(),
        P(),
        P(),
        P(),
        P(),
        P(),
    )
    out_specs = (
        P("wide", "narrow", None, None),
        P("wide", "narrow", None, None),
        P("wide", None),
        P("wide", None),
        P(),
        P(),
        P(),
        P(),
        P(),
        P(),
    )
    return jax.shard_map(
        on_device, mesh=mesh, in_specs=in_specs, out_specs=out_specs, check_vma=False
    )
```

profile of v0, /device:TPU:0, one launch (start us, length us, event | category | flops | bytes accessed | tf_op | source)
XLA Modules:
  0.0 1689.8 jit_solution(10675789634514205833)
XLA Ops:
  18.0 11.4 collective-permute-done
  52.3 13.0 add_convert_fusion.2
  65.3 10.2 reshape.561
  80.8 9.3 all-to-all-start
  94.3 49.7 %all-to-all-done = bf16[4,4,4,16,2304]{4,3,2,0,1:T(8,128)(2,1)} async-done(((bf16[4,4,4,16,2304]{4,3,2,0,1:T(8,128)(2,1)}), bf16[4,4,4,16,2304]{4,3,2,0,1:T(8,128)(2,1)}, u32[]{:S(2)}, u32[]{:S(2)}) %all-to-all-start) | async-done | bytes 4718624 | tf_op jit(solution)/shard_map/all_to_all | solution.py:117
  196.0 14.8 all-to-all-done.1
  243.4 13.1 reshape_reshape.12
  264.2 21.3 %multiply_add_fusion = f32[4,8,32,3072]{3,2,1,0:T(8,128)} fusion(bf16[4,8,32,3072]{3,2,1,0:T(8,128)(2,1)} %copy-done.5, bf16[4,1,32,3072]{3,2,1,0:T(8,128)(2,1)} %collective-permute-done.4, bf16[4,1,32,3072]{3,2,1,0:T(8,128)(2,1)} %collective-permute-done.3, f32[3072]{0:T(1024)S(1)} %bitcast.253, f32[3072]{0:T(1024)S(1)} %bitcast.251, ...), kind=kLoop, calls=%fused_computation.47 | loop fusion | flops 88080384 | bytes 58306560 | tf_op jit(solution)/shard_map/add | solution.py:77
  285.5 45.8 %fusion.9 = (f32[3072]{0:T(1024)}, f32[3072]{0:T(1024)}, f32[3072]{0:T(1024)}, f32[3072]{0:T(1024)}, f32[3072]{0:T(1024)}, /*index=5*/f32[3072]{0:T(1024)}, f32[...) fusion(bf16[4,10,34,3072]{3,2,1,0:T(8,128)(2,1)} %copy-done.3, ...), kind=kOutput, calls=%fused_computation.33 | convolution fusion | flops 4993815552 | bytes 70896656 | tf_op jit(solution)/shard_map/dot_general | solution.py:46
  337.5 13.8 convolution_bitcast_fusion
  357.2 19.0 %add_convert_fusion = bf16[4,8,32,3072]{3,2,1,0:T(8,128)(2,1)} fusion(bf16[4,8,32,3072]{3,2,1,0:T(8,128)(2,1)} %get-tuple-element.103, bf16[4,10,34,3072]{3,2,1,0:T(8,128)(2,1)S(1)} %select_maximum_fusion, bf16[4,1,32,3072]{3,2,1,0:T(8,128)(2,1)S(1)} %collective-permute-done.7, bf16[4,1,32,3072]{3,2,1,0:T(8,128)(2,1)S(1)} %collective-permute-done.8, ...), kind=kLoop, calls=%fused_computation.45 | loop fusion | flops 91226112 | bytes 52015104 | tf_op jit(solution)/shard_map/convert_element_type | solution.py:243
  376.2 9.6 fusion.80
  413.6 10.7 reshape.578
  446.1 9.0 fusion.59
  455.2 10.0 multiply_reduce_fusion
  540.6 38.9 %all-to-all-done.3 = bf16[4,1,16,16,2304]{4,3,0,1,2:T(8,128)(2,1)} async-done(((bf16[4,1,16,16,2304]{4,3,0,1,2:T(8,128)(2,1)}), bf16[4,1,16,16,2304]{4,3,0,1,2:T(8,128)(2,1)}, u32[]{:S(2)}, u32[]{:S(2)}) %all-to-all-start.3) | async-done | bytes 4718624 | tf_op jit(solution)/shard_map/all_to_all | solution.py:126
  579.5 9.4 copy.66
  588.9 10.6 reshape.571
  601.8 21.5 %fusion.21 = (f32[2304]{0:T(1024)S(1)}, f32[2304]{0:T(1024)S(1)}, f32[2304]{0:T(1024)S(1)}, f32[2304]{0:T(1024)S(1)}, f32[2304]{0:T(1024)S(1)}, /*index=5*/f32[2...) fusion(bf16[4,8,32,2304]{3,2,1,0:T(8,128)(2,1)} %reshape.571, ...), kind=kLoop, calls=%fused_computation.58 | loop fusion | flops 70758144 | bytes 39011328 | tf_op jit(solution)/shard_map/srcj,srcj->j/dot_general | solution.py:105
  634.7 14.3 add_convert_fusion.1
  674.3 21.2 %dynamic-update-slice.3 = f32[7126272]{0:T(1024)} dynamic-update-slice(f32[7126272]{0:T(1024)} %constant_dynamic-update-slice_fusion.7, f32[589824]{0:T(1024)} %reshape.575, s32[]{} %constant.134) | dynamic-update-slice | bytes 4718596
  695.5 80.2 %dynamic-update-slice.4 = f32[7126272]{0:T(1024)} dynamic-update-slice(f32[7126272]{0:T(1024)} %dynamic-update-slice.3, f32[2359296]{0:T(1024)} %bitcast.222, s32[]{} %constant.135) | dynamic-update-slice | bytes 18874372
  777.2 80.4 %dynamic-update-slice.6 = f32[7126272]{0:T(1024)} dynamic-update-slice(f32[7126272]{0:T(1024)} %constant_dynamic-update-slice_fusion.6, f32[2359296]{0:T(1024)} %reshape.578, s32[]{} %constant.137) | dynamic-update-slice | bytes 18874372 | tf_op jit(solution)/shard_map/concatenate | solution.py:300
  857.6 472.2 %all-reduce.11 = bf16[7126272]{0:T(1024)(128)(2,1)} all-reduce(f32[7126272]{0:T(1024)} %dynamic-update-slice.6), channel_id=2, replica_groups=mesh['wide'=8,'narrow'=4] {'wide','narrow'}, use_global_device_ids=true, to_apply=%region_19.20.clone | all-reduce | flops 7126272 | bytes 42757632
  1350.9 13.5 multiply_reduce_fusion.1
  1385.5 12.2 all-reduce.6
  1397.6 12.2 collective-permute-done.5
  1409.8 17.3 %collective-permute-done.11 = bf16[2,8,32,768]{3,2,1,0:T(8,128)(2,1)} collective-permute-done((bf16[2,8,32,768]{3,2,1,0:T(8,128)(2,1)}, bf16[2,8,32,768]{3,2,1,0:T(8,128)(2,1)}, u32[]{:S(2)}, u32[]{:S(2)}) %collective-permute-start.11) | collective-permute-done | bytes 786464 | tf_op jit(solution)/shard_map/ppermute | solution.py:29
  1430.3 194.8 %all-reduce.10.cloned.1.call-done = bf16[7126272]{0:T(1024)(128)(2,1)} async-done(((bf16[7126272]{0:T(1024)(128)(2,1)}), bf16[7126272]{0:T(1024)(128)(2,1)}) %all-reduce.10.cloned.1.call-update) | async-done | bytes 14252560
  1650.3 10.1 fusion.82
  1660.4 11.3 slice.404
  1671.7 10.9 reshape.579
  (381 shorter events, 382.1 us)
Async XLA Ops:
  7.2 26.8 %copy-start = (bf16[768,2304]{1,0:T(8,128)(2,1)S(1)}, bf16[768,2304]{1,0:T(8,128)(2,1)}, u32[]{:S(2)}) copy-start(bf16[768,2304]{1,0:T(8,128)(2,1)} %param.16) | copy-start | bytes 10616836
  7.2 22.2 %collective-permute-start = (bf16[2,8,32,768]{3,2,1,0:T(8,128)(2,1)}, bf16[2,8,32,768]{3,2,1,0:T(8,128)(2,1)}, u32[]{:S(2)}, u32[]{:S(2)}) collective-permute-start(bf16[2,8,32,768]{3,2,1,0:T(8,128)(2,1)} %param.11), channel_id=1, source_target_pairs={{0,4},{4,8},{8,12},{12,16},{16,20},{20,24},{24,28},{1,5},{5,9},{9,... | collective-permute-start | bytes 2359304 | tf_op jit(solution)/shard_map/ppermute | solution.py:29
  16.9 22.7 %copy-start.88 = (f32[768]{0:T(1024)}, f32[768]{0:T(1024)S(1)}, u32[]{:S(2)}) copy-start(f32[768]{0:T(1024)S(1)} %get-tuple-element.54) | copy-start | bytes 9220
  16.9 22.7 %copy-start.98 = (f32[768]{0:T(1024)}, f32[768]{0:T(1024)S(1)}, u32[]{:S(2)}) copy-start(f32[768]{0:T(1024)S(1)} %get-tuple-element.53) | copy-start | bytes 9220
  39.7 3.0 collective-permute-start.1
  41.1 5.6 collective-permute-start.2
  80.8 63.2 %all-to-all-start = ((bf16[4,4,4,16,2304]{4,3,2,0,1:T(8,128)(2,1)}), bf16[4,4,4,16,2304]{4,3,2,0,1:T(8,128)(2,1)}, u32[]{:S(2)}, u32[]{:S(2)}) async-start(bf16[4,4,4,16,2304]{4,3,2,0,1:T(8,128)(2,1)} %bitcast.229), calls=%async_computation | async-start | bytes 9437184 | tf_op jit(solution)/shard_map/all_to_all | solution.py:117
  186.4 24.5 %all-to-all-start.1 = ((bf16[4,1,16,16,768]{4,3,0,1,2:T(8,128)(2,1)}), bf16[4,1,16,16,768]{4,3,0,1,2:T(8,128)(2,1)}, u32[]{:S(2)}, u32[]{:S(2)}) async-start(bf16[4,1,16,16,768]{4,3,0,1,2:T(8,128)(2,1)} %copy.51), calls=%async_computation.1 | async-start | bytes 3145728 | tf_op jit(solution)/shard_map/all_to_all | solution.py:126
  190.7 94.7 %collective-permute-start.6 = (bf16[2,8,32,768]{3,2,1,0:T(8,128)(2,1)}, bf16[2,8,32,768]{3,2,1,0:T(8,128)(2,1)}, u32[]{:S(2)}, u32[]{:S(2)}) collective-permute-start(bf16[2,8,32,768]{3,2,1,0:T(8,128)(2,1)} %param.12), channel_id=1, source_target_pairs={{0,4},{4,8},{8,12},{12,16},{16,20},{20,24},{24,28},{1,5},{5,9},{9,... | collective-permute-start | bytes 2359304 | tf_op jit(solution)/shard_map/ppermute | solution.py:29
  226.4 16.3 copy-start.29
  238.3 18.2 %collective-permute-start.3 = (bf16[4,1,32,3072]{3,2,1,0:T(8,128)(2,1)}, bf16[4,1,32,3072]{3,2,1,0:T(8,128)(2,1)}, u32[]{:S(2)}, u32[]{:S(2)}) collective-permute-start(bf16[4,1,32,3072]{3,2,1,0:T(8,128)(2,1)} %get-tuple-element.70), channel_id=1, source_target_pairs={{0,1},{1,2},{2,3},{4,5},{5,6},{6,7},{8,9},{9,10},{10,11},{12,13},{... | collective-permute-start | bytes 2359304 | tf_op jit(solution)/shard_map/ppermute | solution.py:18
  240.7 15.8 collective-permute-start.4
  264.1 21.4 %copy-start.3 = (bf16[4,10,34,3072]{3,2,1,0:T(8,128)(2,1)}, bf16[4,10,34,3072]{3,2,1,0:T(8,128)(2,1)S(1)}, u32[]{:S(2)}) copy-start(bf16[4,10,34,3072]{3,2,1,0:T(8,128)(2,1)S(1)} %select_maximum_fusion.2) | copy-start | bytes 25067524
  332.8 19.2 %collective-permute-start.7 = (bf16[4,1,32,3072]{3,2,1,0:T(8,128)(2,1)S(1)}, bf16[4,1,32,3072]{3,2,1,0:T(8,128)(2,1)S(1)}, u32[]{:S(2)}, u32[]{:S(2)}) collective-permute-start(bf16[4,1,32,3072]{3,2,1,0:T(8,128)(2,1)S(1)} %get-tuple-element.68), channel_id=1, source_target_pairs={{0,1},{1,2},{2,3},{4,5},{5,6},{6,7},{8,9},{9,10},{10,11},{12,13},{... | collective-permute-start | bytes 2359304 | tf_op jit(solution)/shard_map/ppermute | solution.py:18
  335.9 16.1 collective-permute-start.8
  357.2 19.0 %copy-start.7 = (f32[4,8,32,768]{3,2,1,0:T(8,128)S(1)}, f32[4,8,32,768]{3,2,1,0:T(8,128)}, u32[]{:S(2)}) copy-start(f32[4,8,32,768]{3,2,1,0:T(8,128)} %copy-done.6) | copy-start | bytes 9437188
  357.2 19.0 %copy-start.35 = (f32[4,8,32]{2,1,0:T(8,128)S(1)}, f32[4,8,32]{2,1,0:T(8,128)}, u32[]{:S(2)}) copy-start(f32[4,8,32]{2,1,0:T(8,128)} %copy-done.34) | copy-start | bytes 12292
  357.2 19.0 %copy-start.87 = (f32[768]{0:T(1024)S(1)}, f32[768]{0:T(1024)}, u32[]{:S(2)}) copy-start(f32[768]{0:T(1024)} %get-tuple-element.52) | copy-start | bytes 9220
  404.3 27.9 %all-to-all-start.2 = ((bf16[4,4,4,16,768]{4,3,2,0,1:T(8,128)(2,1)}), bf16[4,4,4,16,768]{4,3,2,0,1:T(8,128)(2,1)}, u32[]{:S(2)}, u32[]{:S(2)}) async-start(bf16[4,4,4,16,768]{4,3,2,0,1:T(8,128)(2,1)} %bitcast.235), calls=%async_computation.2 | async-start | bytes 3145728 | tf_op jit(solution)/shard_map/all_to_all | solution.py:117
  446.1 19.1 %slice-start = ((s8[12582912]{0:T(1024)(128)(4,1)}), s8[4194304]{0:T(1024)(128)(4,1)S(1)}, s32[]{:S(2)}) async-start(s8[12582912]{0:T(1024)(128)(4,1)} %bitcast.220), calls=%async_computation.5 | async-start | bytes 8388608
  446.1 19.1 %slice-start.1 = ((s8[12582912]{0:T(1024)(128)(4,1)}), s8[4194304]{0:T(1024)(128)(4,1)S(1)}, s32[]{:S(2)}) async-start(s8[12582912]{0:T(1024)(128)(4,1)} %bitcast.220), calls=%async_computation.6 | async-start | bytes 8388608
  520.7 58.8 %all-to-all-start.3 = ((bf16[4,1,16,16,2304]{4,3,0,1,2:T(8,128)(2,1)}), bf16[4,1,16,16,2304]{4,3,0,1,2:T(8,128)(2,1)}, u32[]{:S(2)}, u32[]{:S(2)}) async-start(bf16[4,1,16,16,2304]{4,3,0,1,2:T(8,128)(2,1)} %copy.64), calls=%async_computation.3 | async-start | bytes 9437184 | tf_op jit(solution)/shard_map/all_to_all | solution.py:126
  525.7 1099.5 %all-reduce.10.cloned.1.call-start = ((), (), s32[]{:S(2)}) async-start(), calls=%async_computation.4 | async-start | bytes 28508160
  623.4 5.8 collective-permute-start.9
  625.5 4.2 collective-permute-start.10
  634.6 16.5 copy-start.13
  634.6 16.5 copy-start.32
  634.6 16.5 copy-start.39
  634.7 16.5 copy-start.89
  634.7 16.5 copy-start.99
  1374.3 35.5 %collective-permute-start.5 = (bf16[2,8,32,768]{3,2,1,0:T(8,128)(2,1)}, bf16[2,8,32,768]{3,2,1,0:T(8,128)(2,1)}, u32[]{:S(2)}, u32[]{:S(2)}) collective-permute-start(bf16[2,8,32,768]{3,2,1,0:T(8,128)(2,1)} %slice.443), channel_id=1, source_target_pairs={{4,0},{8,4},{12,8},{16,12},{20,16},{24,20},{28,24},{5,1},{9,5},{13... | collective-permute-start | bytes 2359304 | tf_op jit(solution)/shard_map/ppermute | solution.py:29
  1375.6 51.5 %collective-permute-start.11 = (bf16[2,8,32,768]{3,2,1,0:T(8,128)(2,1)}, bf16[2,8,32,768]{3,2,1,0:T(8,128)(2,1)}, u32[]{:S(2)}, u32[]{:S(2)}) collective-permute-start(bf16[2,8,32,768]{3,2,1,0:T(8,128)(2,1)} %slice.461), channel_id=1, source_target_pairs={{4,0},{8,4},{12,8},{16,12},{20,16},{24,20},{28,24},{5,1},{9,5},{13... | collective-permute-start | bytes 2359304 | tf_op jit(solution)/shard_map/ppermute | solution.py:29
  (96 other events, 638.2 us)
Sparse Core Ops, SparseCore 0:
  1345.0 280.1 all-reduce.9
where the time goes:
time: 1720 us; the launch traced here: 1690 us
  blocking collectives  484 us (28%)
  local copies, waits for them, and re-layouts  472 us (27%)
  waiting for transfers between devices  344 us (20%)
  matrix products  167 us (10%)
  other arithmetic  156 us (9%)
  starting transfers between devices  51.5 us (3%)
    unnamed x1, blocking collectives  472 us
    unnamed x2, waiting for transfers between devices  195 us
    unnamed x235, local copies, waits for them, and re-layouts  150 us
    concatenate x1, local copies, waits for them, and re-layouts, on_device(): flat = jnp.concatenate([g.reshape(-1) for g in grads])  80.4 us
    dot_general x4, matrix products, project_back(): lax.dot_general(flat, matrix, (((1,), (1,)), ((), ())), preferred_element...  63.9 us
    all_to_all x2, waiting for transfers between devices, to_rows(): lax.all_to_all(split, 'narrow', split_axis=2, concat_axis=1, tiled=True)  53.8 us
    all_to_all x2, waiting for transfers between devices, to_phase(): lax.all_to_all(split, 'narrow', split_axis=1, concat_axis=2, tiled=True)  49.7 us
    slice x9, local copies, waits for them, and re-layouts, on_device(): pieces.append(summed[offset:offset + length].reshape(grad_part.shape))  44.9 us
  transfers between devices with their start and end apart: 17, of which 9 were waited for; matrix products, arithmetic and copies ran while one was open for 10% of the time, Pallas kernels for 0%

commit v1 on v0

v1 whole, which is shorter than its diff:
```python
import functools

import jax
import jax.numpy as jnp
from jax import lax
from jax.experimental import pallas as pl
from jax.experimental.pallas import tpu as pltpu
from jax.sharding import PartitionSpec as P

HEAD_DIM = 64
LANES = 128
GROUPS = 4
MARGIN = 16

masked_score = -1000000000.0
norm_epsilon = 1e-06
gelu_root = 0.7978845608028654
gelu_cube = 0.044715

BF = jnp.bfloat16
F32 = jnp.float32
VMEM_LIMIT = 60 * 1024 * 1024


def dot(left, right, left_dim=1, right_dim=0):
    return lax.dot_general(
        left, right, (((left_dim,), (right_dim,)), ((), ())), preferred_element_type=F32
    )


def iota(shape, dim):
    return lax.broadcasted_iota(jnp.int32, shape, dim)


def phase_rows(rows, start):
    return start + iota((rows, 1), 0)


def live_rows(token, height, breadth):
    row = 2 * ((token >> 4) & 15) + (token >> 9)
    col = 2 * (token & 15) + ((token >> 8) & 1)
    return ((row < height) & (col < breadth)).astype(F32)


def to_phase_matrix():
    row = iota((256, 256), 0)
    col = iota((256, 256), 1)
    grid_row = 2 * ((row >> 4) & 3) + (row >> 7)
    grid_col = 2 * (row & 15) + ((row >> 6) & 1)
    return (col == grid_row * 32 + grid_col).astype(F32).astype(BF)


def normal(values):
    center = values - jnp.mean(values, axis=-1, keepdims=True)
    scale = lax.rsqrt(jnp.mean(center * center, axis=-1, keepdims=True) + norm_epsilon)
    return center * scale, scale


def col_sum(values):
    return jnp.sum(values, axis=0, keepdims=True)


def clear_margins(held):
    zero = jnp.zeros((2 * GROUPS, MARGIN, LANES), F32)
    held[:, 0:MARGIN, :] = zero
    held[:, MARGIN + 256 : 2 * MARGIN + 256, :] = zero


def hold(held, group_of):
    place = iota((256, LANES), 0) & 15
    for g in range(GROUPS):
        values = group_of(g)
        held[2 * g, MARGIN : MARGIN + 256, :] = values
        if g % 2:
            moved = jnp.where(place == 0, 0.0, pltpu.roll(values, 1, 0))
        else:
            moved = jnp.where(place == 15, 0.0, pltpu.roll(values, 255, 0))
        held[2 * g + 1, MARGIN : MARGIN + 256, :] = moved


def taps(g):
    alpha, beta = g // 2, g % 2
    out = []
    for a in range(3):
        for b in range(3):
            row = alpha + a - 1
            col = beta + b - 1
            src = 2 * (row % 2) + col % 2
            out.append((a, b, 2 * src + (0 if 0 <= col <= 1 else 1), MARGIN * (row // 2)))
    return out


STEP = 64


def convolve(held, kernel, write, flip=False):
    weights = [[kernel[3 * a + b : 3 * a + b + 1, :] for b in range(3)] for a in range(3)]

    def at(i, carry):
        start = pl.multiple_of(i * STEP, STEP)
        for g in range(GROUPS):
            total = None
            for a, b, src, off in taps(g):
                weight = weights[2 - a][2 - b] if flip else weights[a][b]
                part = weight * held[src, pl.ds(MARGIN + off + start, STEP), :]
                total = part if total is None else total + part
            write(g, start, total)
        return carry

    lax.fori_loop(0, 256 // STEP, at, 0)


def convolve_back(held, kernel, source, write):
    weights = [[kernel[3 * a + b : 3 * a + b + 1, :] for b in range(3)] for a in range(3)]

    def at(i, sums):
        start = pl.multiple_of(i * STEP, STEP)
        sums = list(sums)
        for g in range(GROUPS):
            total = None
            given = source(g, start)
            for a, b, src, off in taps(g):
                window = held[src, pl.ds(MARGIN + off + start, STEP), :]
                part = weights[2 - a][2 - b] * window
                total = part if total is None else total + part
                at_tap = 3 * (2 - a) + 2 - b
                prod = given * window
                sums[at_tap] = sums[at_tap] + jnp.sum(prod.reshape(STEP // 8, 8, LANES), axis=0)
            write(g, start, total)
        return tuple(sums)

    zero = jnp.zeros((8, LANES), F32)
    sums = lax.fori_loop(0, 256 // STEP, at, (zero,) * 9)
    return jnp.concatenate([col_sum(s) for s in sums], axis=0)


def attend_kernel(
    sc, p0, p1, p2, p3, mod, wq, wk, wv, kq, kk, kv,
    base_out, normed_out, qkv_out, conv_out, prob_out, mixed_out,
    held,
):
    step = pl.program_id(0)
    height, breadth = sc[0], sc[1]

    @pl.when(step == 0)
    def _():
        clear_margins(held)
        shift, scale = mod[0:1, :], 1.0 + mod[1:2, :]
        matrix = to_phase_matrix()
        for k, piece in enumerate((p0, p1, p2, p3)):
            at = sc[2 + k]
            moved = dot(matrix, piece[...])
            for g in range(GROUPS):
                start = pl.multiple_of(g * 256 + at * 64, 64)
                values = moved[g * 64 : g * 64 + 64, :] * live_rows(phase_rows(64, start), height, breadth)
                base_out[pl.ds(start, 64), :] = values.astype(BF)
                normed_out[pl.ds(start, 64), :] = (normal(values)[0] * scale + shift).astype(BF)

    weight = jnp.concatenate([wq[...], wk[...], wv[...]], axis=1)
    for r in range(0, 1024, 512):
        qkv_out[0, r : r + 512, :] = dot(normed_out[r : r + 512, :], weight).astype(BF)
    for s, kernel in enumerate((kq, kk, kv)):
        cols = slice(s * LANES, (s + 1) * LANES)
        hold(held, lambda g: qkv_out[0, g * 256 : g * 256 + 256, cols].astype(F32))

        def write(g, start, total):
            conv_out[0, pl.ds(g * 256 + start, STEP), cols] = total.astype(BF)

        convolve(held, kernel[...].astype(F32), write)

    token = iota((1, 256), 1)
    lane = iota((256, LANES), 1)

    def group(g, carry):
        start = pl.multiple_of(g * 256, 256)
        rows = pl.ds(start, 256)
        live = live_rows(token + start, height, breadth) > 0.5
        query = conv_out[0, rows, 0:LANES] * BF(HEAD_DIM**-0.5)
        key = conv_out[0, rows, LANES : 2 * LANES]
        value = conv_out[0, rows, 2 * LANES : 3 * LANES]
        parts = []
        for h in range(2):
            mine = (lane < HEAD_DIM) if h == 0 else (lane >= HEAD_DIM)
            score = dot(jnp.where(mine, query, BF(0)), key, 1, 1)
            score = jnp.where(live, score, masked_score)
            top = jnp.max(score, axis=-1, keepdims=True)
            raised = jnp.exp(score - top)
            prob = (raised * (1.0 / jnp.sum(raised, axis=-1, keepdims=True))).astype(BF)
            prob_out[0, g, h] = prob
            parts.append(dot(prob, value))
        mixed_out[rows, :] = jnp.where(lane < HEAD_DIM, parts[0], parts[1]).astype(BF)
        return carry

    lax.fori_loop(0, GROUPS, group, 0)


def attend(sc, pieces, mod, qkv_weight, attn_kernel):
    def piece_spec():
        return pl.BlockSpec((256, 768), lambda i, s: (0, 0))

    def weight_spec(k):
        return pl.BlockSpec((768, LANES), lambda i, s: (0, 6 * k + 3 * s[6] + i))

    def kernel_spec(k):
        return pl.BlockSpec((9, LANES), lambda i, s: (0, 6 * k + 3 * s[6] + i))

    whole = pl.BlockSpec((1024, 768), lambda i, s: (0, 0))
    return pl.pallas_call(
        attend_kernel,
        grid_spec=pltpu.PrefetchScalarGridSpec(
            num_scalar_prefetch=1,
            grid=(3,),
            in_specs=[piece_spec() for _ in range(4)]
            + [pl.BlockSpec((8, 768), lambda i, s: (0, 0))]
            + [weight_spec(k) for k in range(3)]
            + [kernel_spec(k) for k in range(3)],
            out_specs=[
                whole,
                whole,
                pl.BlockSpec((1, 1024, 384), lambda i, s: (i, 0, 0)),
                pl.BlockSpec((1, 1024, 384), lambda i, s: (i, 0, 0)),
                pl.BlockSpec((1, GROUPS, 2, 256, 256), lambda i, s: (i, 0, 0, 0, 0)),
                pl.BlockSpec((1024, LANES), lambda i, s: (0, i)),
            ],
            scratch_shapes=[pltpu.VMEM((2 * GROUPS, 2 * MARGIN + 256, LANES), F32)],
        ),
        out_shape=[
            jax.ShapeDtypeStruct((1024, 768), BF),
            jax.ShapeDtypeStruct((1024, 768), BF),
            jax.ShapeDtypeStruct((3, 1024, 384), BF),
            jax.ShapeDtypeStruct((3, 1024, 384), BF),
            jax.ShapeDtypeStruct((3, GROUPS, 2, 256, 256), BF),
            jax.ShapeDtypeStruct((1024, 384), BF),
        ],
        compiler_params=pltpu.CompilerParams(vmem_limit_bytes=VMEM_LIMIT),
        cost_estimate=pl.CostEstimate(flops=3_000_000_000, bytes_accessed=20_000_000, transcendentals=1600000),
        name="attend",
    )(sc, *pieces, mod, qkv_weight, qkv_weight, qkv_weight, attn_kernel, attn_kernel, attn_kernel)


def middle_kernel(
    sc, mixed_own, mixed_other, base, out_weight, mod, c0, c1, c2, c3,
    attended_out, middle_out, normed_out, branch_grad_out, seed_out,
    mixed, attended,
):
    height, breadth, core = sc[0], sc[1], sc[6]
    mixed[:, pl.ds(pl.multiple_of(core * 384, LANES), 384)] = mixed_own[...]
    mixed[:, pl.ds(pl.multiple_of((1 - core) * 384, LANES), 384)] = mixed_other[...]
    for r in range(0, 1024, 512):
        attended[r : r + 512, :] = dot(mixed[r : r + 512, :], out_weight[...])
    gate = mod[2:3, :]
    shift, scale = mod[3:4, :], 1.0 + mod[4:5, :]

    def at(i, carry):
        rows = pl.ds(pl.multiple_of(i * 64, 64), 64)
        got = attended[rows, :]
        attended_out[rows, :] = got.astype(BF)
        middle = base[rows, :].astype(F32) + gate * got
        middle_out[rows, :] = middle
        normed_out[rows, :] = (normal(middle)[0] * scale + shift).astype(BF)
        return carry

    lax.fori_loop(0, 16, at, 0)
    matrix = to_phase_matrix()
    gate_two, factor = mod[5:6, :], mod[6:7, :]
    for k, piece in enumerate((c0, c1, c2, c3)):
        at = sc[2 + k]
        moved = dot(matrix, piece[...])
        for g in range(GROUPS):
            start = pl.multiple_of(g * 256 + at * 64, 64)
            values = moved[g * 64 : g * 64 + 64, :] * live_rows(phase_rows(64, start), height, breadth)
            seed_out[pl.ds(start, 64), :] = values.astype(BF)
            branch_grad_out[pl.ds(start, 64), :] = (values * factor * gate_two).astype(BF)


def project_out(sc, mixed_own, mixed_other, base, out_weight, mod, pieces):
    full = lambda *shape: pl.BlockSpec(shape, lambda i, s: (0,) * len(shape))
    tokens = full(1024, 768)
    return pl.pallas_call(
        middle_kernel,
        grid_spec=pltpu.PrefetchScalarGridSpec(
            num_scalar_prefetch=1,
            grid=(1,),
            in_specs=[full(1024, 384), full(1024, 384), tokens, full(768, 768), full(8, 768)]
            + [full(256, 768)] * 4,
            out_specs=[tokens] * 5,
            scratch_shapes=[pltpu.VMEM((1024, 768), BF), pltpu.VMEM((1024, 768), F32)],
        ),
        out_shape=[
            jax.ShapeDtypeStruct((1024, 768), BF),
            jax.ShapeDtypeStruct((1024, 768), F32),
            jax.ShapeDtypeStruct((1024, 768), BF),
            jax.ShapeDtypeStruct((1024, 768), BF),
            jax.ShapeDtypeStruct((1024, 768), BF),
        ],
        compiler_params=pltpu.CompilerParams(vmem_limit_bytes=VMEM_LIMIT),
        cost_estimate=pl.CostEstimate(flops=2_000_000_000, bytes_accessed=20_000_000, transcendentals=0),
        name="project_out",
    )(sc, mixed_own, mixed_other, base, out_weight, mod, *pieces)


BLOCK = 256


def feed_kernel(
    first, sc, normed, branch_grad, up, down, kernel, *rest,
):
    if first:
        (down_grad, up_grad, kernel_grad, branch_out, normed_grad_out,
         held, normed_t, hid, d_act, acts, d_conv, d_hids) = rest
    else:
        (branch_in, normed_grad_in, down_grad, up_grad, kernel_grad, branch_out, normed_grad_out,
         held, normed_t, hid, d_act, acts, d_conv, d_hids) = rest
    step = pl.program_id(0)

    @pl.when(step == 0)
    def _():
        clear_margins(held)
        for r in range(0, 1024, 256):
            normed_t[:, r : r + 256] = normed[r : r + 256, :].T

    block = pl.ds(pl.multiple_of(step * BLOCK, BLOCK), BLOCK)
    for r in range(0, 1024, 512):
        hid[r : r + 512, :] = dot(normed[r : r + 512, :], up[:, block]).astype(BF)
        d_act[r : r + 512, :] = dot(branch_grad[r : r + 512, :], down[block, :], 1, 1)
    for lane_block in range(BLOCK // LANES):
        cols = slice(lane_block * LANES, (lane_block + 1) * LANES)
        dest = pl.ds(pl.multiple_of(step * BLOCK + lane_block * LANES, LANES), LANES)
        weights = kernel[:, cols].astype(F32)
        hold(held, lambda g: hid[g * 256 : g * 256 + 256, cols].astype(F32))

        def activate(g, start, v):
            rows = pl.ds(g * 256 + start, STEP)
            square = v * v
            bent = jnp.tanh(gelu_root * v * (1.0 + gelu_cube * square))
            half = 0.5 + 0.5 * bent
            acts[rows, dest] = (v * half).astype(BF)
            slope = half + 0.5 * v * (1.0 - bent * bent) * (gelu_root + 3.0 * gelu_root * gelu_cube * square)
            d_conv[rows, :] = (d_act[rows, cols] * slope).astype(BF)

        convolve(held, weights, activate)
        hold(held, lambda g: d_conv[g * 256 : g * 256 + 256, :].astype(F32))

        def source(g, start):
            return hid[pl.ds(g * 256 + start, STEP), cols].astype(F32)

        def write(g, start, total):
            d_hids[pl.ds(g * 256 + start, STEP), dest] = total.astype(BF)

        kernel_grad[:, cols] = convolve_back(held, weights, source, write)
    down_grad[block, :] = dot(acts[:, block].T, branch_grad[...]).astype(BF)
    up_grad[:, block] = dot(normed_t[...], d_hids[:, block]).astype(BF)

    @pl.when(step == pl.num_programs(0) - 1)
    def _():
        for r in range(0, 1024, 512):
            rows = slice(r, r + 512)
            branch = dot(acts[rows, :], down[...])
            normed_grad = dot(d_hids[rows, :], up[...], 1, 1)
            if not first:
                branch = branch + branch_in[rows, :]
                normed_grad = normed_grad + normed_grad_in[rows, :]
            branch_out[rows, :] = branch
            normed_grad_out[rows, :] = normed_grad


def feed(sc, normed, branch_grad, up_weight, down_weight, ffn_kernel, half, before):
    full = lambda *shape: pl.BlockSpec(shape, lambda i, s: (0,) * len(shape))
    tokens = full(1024, 768)
    first = before is None
    return pl.pallas_call(
        functools.partial(feed_kernel, first),
        grid_spec=pltpu.PrefetchScalarGridSpec(
            num_scalar_prefetch=1,
            grid=(3,),
            in_specs=[
                tokens,
                tokens,
                pl.BlockSpec((768, 768), lambda i, s: (0, 2 * s[6] + half)),
                pl.BlockSpec((768, 768), lambda i, s: (2 * s[6] + half, 0)),
                pl.BlockSpec((9, BLOCK), lambda i, s: (0, 6 * s[6] + 3 * half + i)),
            ]
            + ([] if first else [tokens, tokens]),
            out_specs=[
                full(768, 768),
                full(768, 768),
                pl.BlockSpec((9, BLOCK), lambda i, s: (0, i)),
                tokens,
                tokens,
            ],
            scratch_shapes=[
                pltpu.VMEM((2 * GROUPS, 2 * MARGIN + 256, LANES), F32),
                pltpu.VMEM((768, 1024), BF),
                pltpu.VMEM((1024, BLOCK), BF),
                pltpu.VMEM((1024, BLOCK), F32),
                pltpu.VMEM((1024, 768), BF),
                pltpu.VMEM((1024, LANES), BF),
                pltpu.VMEM((1024, 768), BF),
            ],
        ),
        out_shape=[
            jax.ShapeDtypeStruct((768, 768), BF),
            jax.ShapeDtypeStruct((768, 768), BF),
            jax.ShapeDtypeStruct((9, 768), F32),
            jax.ShapeDtypeStruct((1024, 768), F32),
            jax.ShapeDtypeStruct((1024, 768), F32),
        ],
        compiler_params=pltpu.CompilerParams(vmem_limit_bytes=VMEM_LIMIT),
        cost_estimate=pl.CostEstimate(flops=7_500_000_000, bytes_accessed=20_000_000, transcendentals=800000),
        name="feed",
    )(sc, normed, branch_grad, up_weight, down_weight, ffn_kernel, *([] if first else before))


def finish_kernel(sc, middle, branch, branch_other, seed, mod, near_out, far_out, sums_out):
    height, breadth, core = sc[0], sc[1], sc[6]
    gate, factor = mod[5:6, :], mod[6:7, :]
    matrix = to_phase_matrix()
    total = jnp.zeros((1, 768), F32)
    for local in range(2):
        parts = []
        for g in range(GROUPS):
            token = phase_rows(64, g * 256 + (2 * local + core) * 64)
            whole = branch[2 * g + local, 0] + branch_other[2 * g + local].astype(F32)
            total = total + col_sum(seed[2 * g + local, 0].astype(F32) * whole)
            result = middle[2 * g + local, 0] + gate * whole
            parts.append((result * live_rows(token, height, breadth)).astype(BF))
        done = dot(matrix, jnp.concatenate(parts, axis=0), 0, 0).astype(BF)

        @pl.when(sc[7] == local)
        def _():
            near_out[...] = done

        @pl.when(sc[7] != local)
        def _():
            far_out[...] = done

    sums_out[...] = total * factor


def half_spec():
    return pl.BlockSpec((8, 1, 64, 768), lambda i, s: (0, s[6], 0, 0))


def finish(sc, middle, branch, branch_other, seed, mod):
    full = lambda *shape: pl.BlockSpec(shape, lambda i, s: (0,) * len(shape))
    halves = lambda v: v.reshape(8, 2, 64, 768)
    return pl.pallas_call(
        finish_kernel,
        grid_spec=pltpu.PrefetchScalarGridSpec(
            num_scalar_prefetch=1,
            grid=(1,),
            in_specs=[half_spec(), half_spec(), full(8, 64, 768), half_spec(), full(8, 768)],
            out_specs=[full(256, 768), full(256, 768), full(1, 768)],
        ),
        out_shape=[
            jax.ShapeDtypeStruct((256, 768), BF),
            jax.ShapeDtypeStruct((256, 768), BF),
            jax.ShapeDtypeStruct((1, 768), F32),
        ],
        compiler_params=pltpu.CompilerParams(vmem_limit_bytes=VMEM_LIMIT),
        cost_estimate=pl.CostEstimate(flops=300_000_000, bytes_accessed=6_000_000, transcendentals=0),
        name="finish",
    )(sc, halves(middle), halves(branch), branch_other, halves(seed), mod)


def attend_back_kernel(
    sc, normed_grad, normed_grad_other, middle, attended, seed, mod,
    mixed, out_weight, normed, qkv, conv, prob, wq, wk, wv, kq, kk, kv,
    middle_grad, sums_out, weight_grad, kernel_grad, normed_grad_out,
    held, normed_t, d_att, d_mixed, d_conv, d_qkv,
):
    step = pl.program_id(0)

    @pl.when(step == 0)
    def _():
        clear_margins(held)
        for r in range(0, 1024, 256):
            normed_t[:, r : r + 256] = normed[r : r + 256, :].T
        gate, scale, factor = mod[2:3, :], 1.0 + mod[4:5, :], mod[6:7, :]

        def at(i, sums):
            d_shift, d_scale, d_gate = sums
            rows = pl.ds(pl.multiple_of(i * 64, 64), 64)
            grad = normed_grad[rows, :] + normed_grad_other[rows, :].astype(F32)
            unit, inverse = normal(middle[rows, :])
            both = grad * unit
            d_shift = d_shift + col_sum(grad)
            d_scale = d_scale + col_sum(both)
            grad = grad * scale
            mean = jnp.mean(grad, axis=-1, keepdims=True)
            along = jnp.mean(both * scale, axis=-1, keepdims=True)
            total = seed[rows, :].astype(F32) * factor + inverse * (grad - mean - unit * along)
            middle_grad[rows, :] = total
            d_gate = d_gate + col_sum(total * attended[rows, :].astype(F32))
            d_att[rows, :] = (total * gate).astype(BF)
            return d_shift, d_scale, d_gate

        zero = jnp.zeros((1, 768), F32)
        sums = lax.fori_loop(0, 16, at, (zero, zero, zero))
        for k in range(3):
            sums_out[k : k + 1, :] = 0.5 * sums[k]
        mixed_t = mixed[...].T
        grad = dot(mixed_t, d_att[...]).astype(BF)
        weight_grad[0:384, 1152:1536] = grad[:, 0:384]
        weight_grad[384:768, 1152:1536] = grad[:, 384:768]

    for r in range(0, 1024, 512):
        d_mixed[r : r + 512, :] = dot(d_att[r : r + 512, :], out_weight[...], 1, 1).astype(BF)

    lane = iota((256, LANES), 1)

    def group(g, carry):
        rows = pl.ds(pl.multiple_of(g * 256, 256), 256)
        grad = d_mixed[rows, :]
        query = conv[0, rows, 0:LANES]
        key = conv[0, rows, LANES : 2 * LANES]
        value = conv[0, rows, 2 * LANES : 3 * LANES]
        parts = []
        for h in range(2):
            mine = (lane < HEAD_DIM) if h == 0 else (lane >= HEAD_DIM)
            p = prob[0, g, h]
            d_value = dot(p.T, grad)
            d_prob = dot(jnp.where(mine, grad, BF(0)), value, 1, 1)
            wide_p = p.astype(F32)
            inner = jnp.sum(d_prob * wide_p, axis=-1, keepdims=True)
            d_score = (wide_p * (d_prob - inner)).astype(BF)
            parts.append((dot(d_score, key), dot(d_score.T, query), d_value))
        low = lane < HEAD_DIM
        for k in range(3):
            picked = jnp.where(low, parts[0][k], parts[1][k])
            if k < 2:
                picked = picked * HEAD_DIM**-0.5
            d_conv[rows, k * LANES : (k + 1) * LANES] = picked.astype(BF)
        return carry

    lax.fori_loop(0, GROUPS, group, 0)
    for s, kernel in enumerate((kq, kk, kv)):
        cols = slice(s * LANES, (s + 1) * LANES)
        hold(held, lambda g: d_conv[g * 256 : g * 256 + 256, cols].astype(F32))

        def source(g, start):
            return qkv[0, pl.ds(g * 256 + start, STEP), cols].astype(F32)

        def write(g, start, total):
            d_qkv[pl.ds(g * 256 + start, STEP), cols] = total.astype(BF)

        kernel_grad[0, :, cols] = convolve_back(held, kernel[...].astype(F32), source, write)
    grad = dot(normed_t[...], d_qkv[...]).astype(BF)
    for s in range(3):
        dest = pl.ds(pl.multiple_of(s * 384 + step * LANES, LANES), LANES)
        weight_grad[:, dest] = grad[:, s * LANES : (s + 1) * LANES]
    weight = jnp.concatenate([wq[...], wk[...], wv[...]], axis=1)
    for r in range(0, 1024, 512):
        part = dot(d_qkv[r : r + 512, :], weight, 1, 1)

        @pl.when(step == 0)
        def _():
            normed_grad_out[r : r + 512, :] = part

        @pl.when(step != 0)
        def _():
            normed_grad_out[r : r + 512, :] += part


def attend_back(sc, normed_grad, normed_grad_other, middle, attended, seed, mod, mixed, out_weight,
                normed, qkv, conv, prob, qkv_weight, attn_kernel):
    full = lambda *shape: pl.BlockSpec(shape, lambda i, s: (0,) * len(shape))
    tokens = full(1024, 768)

    def weight_spec(k):
        return pl.BlockSpec((768, LANES), lambda i, s: (0, 6 * k + 3 * s[6] + i))

    def kernel_spec(k):
        return pl.BlockSpec((9, LANES), lambda i, s: (0, 6 * k + 3 * s[6] + i))

    saved = pl.BlockSpec((1, 1024, 384), lambda i, s: (i, 0, 0))
    return pl.pallas_call(
        attend_back_kernel,
        grid_spec=pltpu.PrefetchScalarGridSpec(
            num_scalar_prefetch=1,
            grid=(3,),
            in_specs=[tokens, tokens, tokens, tokens, tokens, full(8, 768), full(1024, 384),
                      pl.BlockSpec((LANES, 768), lambda i, s: (3 * s[6] + i, 0)),
                      tokens, saved, saved,
                      pl.BlockSpec((1, GROUPS, 2, 256, 256), lambda i, s: (i, 0, 0, 0, 0))]
            + [weight_spec(k) for k in range(3)]
            + [kernel_spec(k) for k in range(3)],
            out_specs=[
                tokens,
                full(3, 768),
                full(768, 1536),
                pl.BlockSpec((1, 9, 384), lambda i, s: (i, 0, 0)),
                tokens,
            ],
            scratch_shapes=[
                pltpu.VMEM((2 * GROUPS, 2 * MARGIN + 256, LANES), F32),
                pltpu.VMEM((768, 1024), BF),
                pltpu.VMEM((1024, 768), BF),
                pltpu.VMEM((1024, LANES), BF),
                pltpu.VMEM((1024, 384), BF),
                pltpu.VMEM((1024, 384), BF),
            ],
        ),
        out_shape=[
            jax.ShapeDtypeStruct((1024, 768), F32),
            jax.ShapeDtypeStruct((3, 768), F32),
            jax.ShapeDtypeStruct((768, 1536), BF),
            jax.ShapeDtypeStruct((3, 9, 384), F32),
            jax.ShapeDtypeStruct((1024, 768), F32),
        ],
        compiler_params=pltpu.CompilerParams(vmem_limit_bytes=VMEM_LIMIT),
        cost_estimate=pl.CostEstimate(flops=8_000_000_000, bytes_accessed=30_000_000, transcendentals=0),
        name="attend_back",
    )(sc, normed_grad, normed_grad_other, middle, attended, seed, mod, mixed, out_weight,
      normed, qkv, conv, prob, qkv_weight, qkv_weight, qkv_weight, attn_kernel, attn_kernel, attn_kernel)


def input_kernel(sc, grad, grad_other, middle_grad, base, mod, near_out, far_out, sums_out):
    height, breadth, core = sc[0], sc[1], sc[6]
    scale = 1.0 + mod[1:2, :]
    matrix = to_phase_matrix()
    d_shift = jnp.zeros((1, 768), F32)
    d_scale = jnp.zeros((1, 768), F32)
    for local in range(2):
        parts = []
        for g in range(GROUPS):
            at = 2 * g + local
            token = phase_rows(64, g * 256 + (2 * local + core) * 64)
            total = grad[at, 0] + grad_other[at].astype(F32)
            unit, inverse = normal(base[at, 0].astype(F32))
            both = total * unit
            d_shift = d_shift + col_sum(total)
            d_scale = d_scale + col_sum(both)
            total = total * scale
            mean = jnp.mean(total, axis=-1, keepdims=True)
            along = jnp.mean(both * scale, axis=-1, keepdims=True)
            total = middle_grad[at, 0] + inverse * (total - mean - unit * along)
            parts.append((total * live_rows(token, height, breadth)).astype(BF))
        done = dot(matrix, jnp.concatenate(parts, axis=0), 0, 0).astype(BF)

        @pl.when(sc[7] == local)
        def _():
            near_out[...] = done

        @pl.when(sc[7] != local)
        def _():
            far_out[...] = done

    sums_out[0:1, :] = d_shift
    sums_out[1:2, :] = d_scale


def input_grad(sc, grad, grad_other, middle_grad, base, mod):
    full = lambda *shape: pl.BlockSpec(shape, lambda i, s: (0,) * len(shape))
    halves = lambda v: v.reshape(8, 2, 64, 768)
    return pl.pallas_call(
        input_kernel,
        grid_spec=pltpu.PrefetchScalarGridSpec(
            num_scalar_prefetch=1,
            grid=(1,),
            in_specs=[half_spec(), full(8, 64, 768), half_spec(), half_spec(), full(8, 768)],
            out_specs=[full(256, 768), full(256, 768), full(2, 768)],
        ),
        out_shape=[
            jax.ShapeDtypeStruct((256, 768), BF),
            jax.ShapeDtypeStruct((256, 768), BF),
            jax.ShapeDtypeStruct((2, 768), F32),
        ],
        compiler_params=pltpu.CompilerParams(vmem_limit_bytes=VMEM_LIMIT),
        cost_estimate=pl.CostEstimate(flops=300_000_000, bytes_accessed=6_000_000, transcendentals=0),
        name="input_grad",
    )(sc, halves(grad), grad_other, halves(middle_grad), halves(base), mod)


def swap(values, axis, bit):
    count = lax.axis_size(axis)
    return lax.ppermute(values, axis, [(i, i ^ bit) for i in range(count)])


def bits_of(count):
    return [1 << k for k in range(count.bit_length() - 1)]


def halving_order():
    wide = [("wide", bit) for bit in bits_of(lax.axis_size("wide"))]
    return wide


def has_bit(axis, bit):
    return (lax.axis_index(axis) & bit) != 0


def scatter_sum(block, order):
    for axis, bit in order:
        high = has_bit(axis, bit)
        half = block.shape[0] // 2
        lower, upper = block[:half], block[half:]
        send = jnp.where(high, lower, upper)
        keep = jnp.where(high, upper, lower)
        got = swap(send, axis, bit)
        block = (keep.astype(F32) + got.astype(F32)).astype(BF)
    return block


def gather(block, order):
    for axis, bit in reversed(order):
        got = swap(block, axis, bit)
        high = has_bit(axis, bit)
        block = jnp.concatenate([jnp.where(high, got, block), jnp.where(high, block, got)], axis=0)
    return block


def sum_all(values, order):
    for axis, bit in order:
        values = values + swap(values, axis, bit)
    return values


def on_device(
    tokens, cotangent, conditioning, aspect, bucket,
    qkv_weight, attn_kernel, out_weight, up_weight, ffn_kernel, down_weight,
):
    wide_count = lax.axis_size("wide")
    wide_at = lax.axis_index("wide")
    narrow_at = lax.axis_index("narrow")
    pair, core = narrow_at // 2, narrow_at % 2
    item = 2 * wide_at + pair
    sides = lax.dynamic_index_in_dim(aspect, item, 0, keepdims=False)
    home = lax.dynamic_index_in_dim(bucket, item, 0, keepdims=False)
    stays = home == wide_at

    def pieces_of(block):
        flat = block.reshape(2, 256, 768)
        own = lax.dynamic_index_in_dim(flat, pair, 0, keepdims=False)
        far = lax.dynamic_index_in_dim(flat, 1 - pair, 0, keepdims=False)
        got = swap(far, "narrow", 2)
        return own, got, swap(own, "narrow", 1), swap(got, "narrow", 1)

    token_pieces = pieces_of(tokens)
    seed_pieces = pieces_of(cotangent)
    from_right = lax.ppermute(conditioning, "wide", [(i + 1, i) for i in range(wide_count - 1)])
    modul = jnp.where(stays, conditioning, from_right).astype(F32).reshape(6, 768)
    factor = 1024.0 / (sides[0] * sides[1]).astype(F32)
    mod = jnp.concatenate([modul, jnp.full((2, 768), factor, F32)], axis=0)
    sc = jnp.stack(
        [sides[0], sides[1], 2 * pair + core, 2 * (1 - pair) + core, 2 * pair + 1 - core,
         2 * (1 - pair) + 1 - core, core, pair]
    ).astype(jnp.int32)
    attn_k = attn_kernel.reshape(9, -1)
    ffn_k = ffn_kernel.reshape(9, -1)

    base, normed_one, qkv, conv, prob, mixed = attend(sc, token_pieces, mod, qkv_weight, attn_k)
    mixed_other = swap(mixed, "narrow", 1)
    attended, middle, normed_two, d_branch, seed = project_out(
        sc, mixed, mixed_other, base, out_weight, mod, seed_pieces
    )
    down_a, up_a, ffn_a, branch, d_normed = feed(
        sc, normed_two, d_branch, up_weight, down_weight, ffn_k, 0, None
    )
    down_b, up_b, ffn_b, branch, d_normed = feed(
        sc, normed_two, d_branch, up_weight, down_weight, ffn_k, 1, (branch, d_normed)
    )

    def other_half(values):
        cut = values.reshape(8, 2, 64, 768)
        return lax.dynamic_index_in_dim(cut, 1 - core, 1, keepdims=False).astype(BF)

    d_normed_other = swap(d_normed.astype(BF), "narrow", 1)
    branch_other = swap(other_half(branch), "narrow", 1)
    near, far, d_gate_two = finish(sc, middle, branch, branch_other, seed, mod)
    far = swap(far, "narrow", 2)

    def as_output(near, far):
        first = jnp.where(pair == 0, near, far)
        second = jnp.where(pair == 0, far, near)
        return jnp.stack([first, second]).reshape(tokens.shape)

    block_out = as_output(near, far)
    d_middle, sums_two, attn_bundle, attn_kg, d_first = attend_back(
        sc, d_normed, d_normed_other, middle, attended, seed, mod, mixed, out_weight,
        normed_one, qkv, conv, prob, qkv_weight, attn_k
    )
    d_first_other = swap(other_half(d_first), "narrow", 1)
    near, far, sums_one = input_grad(sc, d_first, d_first_other, d_middle, base, mod)
    tokens_grad = as_output(near, swap(far, "narrow", 2))

    cond = jnp.concatenate(
        [sums_one, sums_two[2:3], sums_two[1:2], d_gate_two, sums_two[0:1]], axis=0
    )
    moves = jnp.where(stays, 0.0, cond)
    cond = jnp.where(stays, cond, 0.0) + lax.ppermute(
        moves, "wide", [(i, i + 1) for i in range(wide_count - 1)]
    )
    cond = sum_all(cond, [("narrow", 1), ("narrow", 2)])

    chips = [("wide", bit) for bit in bits_of(wide_count)] + [("narrow", 2)]
    order = [("narrow", 2)] + [("wide", bit) for bit in bits_of(wide_count)]

    def reduce(block):
        half = gather(scatter_sum(block, order), order)
        other = swap(half, "narrow", 1)
        return jnp.where(core == 0, half, other), jnp.where(core == 0, other, half)

    down_a0, down_a1 = reduce(down_a)
    up_a0, up_a1 = reduce(up_a)
    down_b0, down_b1 = reduce(down_b)
    up_b0, up_b1 = reduce(up_b)
    attn0, attn1 = reduce(attn_bundle)
    down_grad = jnp.concatenate([down_a0, down_b0, down_a1, down_b1], axis=0).astype(F32)
    up_grad = jnp.concatenate([up_a0, up_b0, up_a1, up_b1], axis=1).astype(F32)
    qkv_grad = jnp.concatenate(
        [v[:, 384 * s : 384 * s + 384] for s in range(3) for v in (attn0, attn1)], axis=1
    ).astype(F32)
    out_grad = jnp.concatenate(
        [
            jnp.concatenate([v[0:384, 1152:], v[384:768, 1152:]], axis=1)
            for v in (attn0, attn1)
        ],
        axis=0,
    ).astype(F32)

    def kernel_grads(values):
        half = sum_all(values, chips)
        other = swap(half, "narrow", 1)
        return jnp.where(core == 0, half, other), jnp.where(core == 0, other, half)

    ffn0, ffn1 = kernel_grads(jnp.concatenate([ffn_a, ffn_b], axis=1))
    ffn_grad = jnp.concatenate([ffn0, ffn1], axis=1).reshape(ffn_kernel.shape)
    attn_kg = attn_kg.reshape(3, 9, 3, 128).transpose(1, 2, 0, 3).reshape(9, 3, 384)
    kg0, kg1 = kernel_grads(attn_kg)
    attn_grad = jnp.concatenate([kg0, kg1], axis=2).reshape(attn_kernel.shape)

    return (
        block_out, tokens_grad, cond[0:5].reshape(1, -1), cond[5:6],
        qkv_grad, attn_grad, out_grad, up_grad, ffn_grad, down_grad,
    )


def solution(mesh):
    rows = P("wide", "narrow", None, None)
    in_specs = (rows, rows, P("wide", None)) + (P(),) * 8
    out_specs = (rows, rows, P("wide", None), P("wide", None)) + (P(),) * 6
    return jax.shard_map(
        on_device, mesh=mesh, in_specs=in_specs, out_specs=out_specs, check_vma=False
    )
```

time: 1720 us -> 474 us (0.28); the launches traced: 1690 us -> 464 us
  blocking collectives: 484 us -> 0 us
  local copies, waits for them, and re-layouts: 472 us -> 21.6 us
  waiting for transfers between devices: 344 us -> 174 us
  matrix products: 167 us -> 0 us
  Pallas kernels: 0 us -> 147 us
  other arithmetic: 156 us -> 62.1 us
    unnamed x1 -> x0, blocking collectives: 472 us -> none
    unnamed x2 -> x0, waiting for transfers between devices: 195 us -> none
    dot_general x18 -> x0, matrix products: 167 us -> none  [the longest x4 63.9 us: project_back(): lax.dot_general(flat, matrix, (((1,), (1,)), ((), ())), preferred_element...]
    pallas_call x0 -> x7, Pallas kernels: none -> 147 us  [the longest x2 53.2 us: feed(): pl.pallas_call(functools.partial(feed_kernel, first), grid_spec=pltpu.Pre...]
    unnamed x235 -> x90, local copies, waits for them, and re-layouts: 150 us -> 5.9 us
    ppermute x12 -> x71, waiting for transfers between devices: 45.4 us -> 174 us  [the longest x69 174 us: swap(): return lax.ppermute(values, axis, [(i, i ^ bit) for i in range(count)])]
    all_to_all x4 -> x0, waiting for transfers between devices: 103 us -> none  [the longest x2 53.8 us: to_rows(): lax.all_to_all(split, 'narrow', split_axis=2, concat_axis=1, tiled=True)]
    concatenate x6 -> x4, local copies, waits for them, and re-layouts: 103 us -> 2.83 us  [the longest x1 1.32 us: on_device(): jnp.concatenate([sums_one, sums_two[2:3], sums_two[1:2], d_gate_two, sums...]
  transfers between devices with their start and end apart: 17 -> 71, of which waited for: 9 -> 35; matrix products, arithmetic and copies ran while one was open for 10% -> 15% of each run, Pallas kernels for 0% -> 18%
where the time goes in v1:
time: 474 us; the launch traced here: 464 us
  waiting for transfers between devices  174 us (37%)
  Pallas kernels  147 us (31%)
  other arithmetic  62.1 us (13%)
  starting transfers between devices  55 us (12%)
  local copies, waits for them, and re-layouts  21.6 us (5%)
    ppermute x69, waiting for transfers between devices, swap(): return lax.ppermute(values, axis, [(i, i ^ bit) for i in range(count)])  174 us
    pallas_call x2, Pallas kernels, feed(): pl.pallas_call(functools.partial(feed_kernel, first), grid_spec=pltpu.Pre...  53.2 us
    ppermute x69, starting transfers between devices, swap(): return lax.ppermute(values, axis, [(i, i ^ bit) for i in range(count)])  50 us
    pallas_call x1, Pallas kernels, attend_back(): pl.pallas_call(attend_back_kernel, grid_spec=pltpu.PrefetchScalarGridSpec...  45.2 us
    pallas_call x1, Pallas kernels, attend(): pl.pallas_call(attend_kernel, grid_spec=pltpu.PrefetchScalarGridSpec(num_...  24.8 us
    pallas_call x1, Pallas kernels, project_out(): pl.pallas_call(middle_kernel, grid_spec=pltpu.PrefetchScalarGridSpec(num_...  12.6 us
    select_n x20, other arithmetic, gather(): jnp.where(high, got, block)  10.5 us
  transfers between devices with their start and end apart: 71, of which 35 were waited for; matrix products, arithmetic and copies ran while one was open for 15% of the time, Pallas kernels for 18%

profile of v1, /device:TPU:0, one launch (start us, length us, event | category | flops | bytes accessed | tf_op | source)
XLA Modules:
  0.0 464.4 jit_solution(1839387650091191004)
XLA Ops:
  2.0 3.0 collective-permute-start
  6.3 7.8 %collective-permute-done.p1 = bf16[256,768]{1,0:T(8,128)(2,1)S(1)} collective-permute-done((bf16[256,768]{1,0:T(8,128)(2,1)S(1)}, bf16[256,768]{1,0:T(8,128)(2,1)S(1)}, u32[]{:S(2)}, u32[]{:S(2)}) %collective-permute-start) | collective-permute-done | bytes 393248 | tf_op jit(solution)/shard_map/ppermute | solution.py:677
  23.9 24.8 %attend.1 = (bf16[1024,768]{1,0:T(8,128)(2,1)}, bf16[1024,768]{1,0:T(8,128)(2,1)}, bf16[3,1024,384]{2,1,0:T(8,128)(2,1)}, bf16[3,1024,384]{2,1,0:T(8,128)(2,1)},...) custom-call(s32[8]{0:T(128)} %stack.45.sc, bf16[256,768]{1,0:T(8,128)(2,1)} %copy-done.18, ...), custom_call_target="tpu_custom_call" | custom-call | flops 3000000000 | bytes 20000000 | tf_op jit(solution)/shard_map/attend/pallas_call | solution.py:208
  53.4 12.6 %project_out.1 = (bf16[1024,768]{1,0:T(8,128)(2,1)}, f32[1024,768]{1,0:T(8,128)}, bf16[1024,768]{1,0:T(8,128)(2,1)}, bf16[1024,768]{1,0:T(8,128)(2,1)}, bf16[1024,768]{1,0:T(8,128)(2,1)}) custom-call(s32[8]{0:T(128)} %stack.45.sc, bf16[1024,384]{1,0:T(8,128)(2,1)} %get-tuple-element.42.mixed_own.mixed, bf16[1024,384]{1,0:T(8,128)(2,1)} %copy-done.36, ...), custom_call_target="tpu_custom_call" | custom-call | flops 2000000000 | bytes 20000000 | tf_op jit(solution)/shard_map/project_out/pallas_call | solution.py:279
  66.0 25.6 %feed.2 = (bf16[768,768]{1,0:T(8,128)(2,1)}, bf16[768,768]{1,0:T(8,128)(2,1)}, f32[9,768]{1,0:T(8,128)}, f32[1024,768]{1,0:T(8,128)}, f32[1024,768]{1,0:T(8,128)}) custom-call(s32[8]{0:T(128)} %stack.45.sc, bf16[1024,768]{1,0:T(8,128)(2,1)} %get-tuple-element.45.normed, bf16[1024,768]{1,0:T(8,128)(2,1)} %get-tuple-element.46.branch_grad, ...), custom_call_target="tpu_custom_call" | custom-call | flops 7500000256 | bytes 20000000 | tf_op jit(solution)/shard_map/feed/pallas_call | solution.py:371
  92.3 27.6 %feed.3 = (bf16[768,768]{1,0:T(8,128)(2,1)}, bf16[768,768]{1,0:T(8,128)(2,1)}, f32[9,768]{1,0:T(8,128)}, f32[1024,768]{1,0:T(8,128)}, f32[1024,768]{1,0:T(8,128)}) custom-call(s32[8]{0:T(128)} %stack.45.sc, bf16[1024,768]{1,0:T(8,128)(2,1)} %get-tuple-element.45.normed, bf16[1024,768]{1,0:T(8,128)(2,1)} %get-tuple-element.46.branch_grad, ...), custom_call_target="tpu_custom_call" | custom-call | flops 7500000256 | bytes 20000000 | tf_op jit(solution)/shard_map/feed/pallas_call | solution.py:371
  124.6 3.3 convert_element_type.215
  133.3 2.7 collective-permute-start.50
  137.4 2.8 collective-permute-done.50
  141.8 19.2 %collective-permute-done.51 = f32[9,1536]{1,0:T(8,128)S(1)} collective-permute-done((f32[9,1536]{1,0:T(8,128)S(1)}, f32[9,1536]{1,0:T(8,128)S(1)}, u32[]{:S(2)}, u32[]{:S(2)}) %collective-permute-start.51) | collective-permute-done | bytes 55328 | tf_op jit(solution)/shard_map/ppermute | solution.py:677
  169.9 8.9 %collective-permute-done.62 = bf16[384,768]{1,0:T(8,128)(2,1)} collective-permute-done((bf16[384,768]{1,0:T(8,128)(2,1)}, bf16[384,768]{1,0:T(8,128)(2,1)}, u32[]{:S(2)}, u32[]{:S(2)}) %collective-permute-start.62) | collective-permute-done | bytes 589856 | tf_op jit(solution)/shard_map/ppermute | solution.py:677
  181.3 9.2 %collective-permute-done.53 = bf16[384,768]{1,0:T(8,128)(2,1)S(1)} collective-permute-done((bf16[384,768]{1,0:T(8,128)(2,1)}, bf16[384,768]{1,0:T(8,128)(2,1)S(1)}, u32[]{:S(2)}, u32[]{:S(2)}) %collective-permute-start.53) | collective-permute-done | bytes 589856 | tf_op jit(solution)/shard_map/ppermute | solution.py:677
  192.9 5.0 %finish.1 = (bf16[256,768]{1,0:T(8,128)(2,1)}, bf16[256,768]{1,0:T(8,128)(2,1)}, f32[1,768]{1,0:T(1,128)}) custom-call(s32[8]{0:T(128)} %stack.45.sc, f32[8,2,64,768]{3,2,1,0:T(8,128)} %bitcast.53, f32[8,2,64,768]{3,2,1,0:T(8,128)} %bitcast.58, bf16[8,64,768]{2,1,0:T(8,128)(2,1)} %collective-permute-done.8.branch_other, bf16[8,2,64,768]{3,2,1,0:T(8,128)(2,1)} %bitcast.54, ...), custom_call_target="tpu_custom_call" | custom-call | flops 300000000 | bytes 6000000 | tf_op jit(solution)/shard_map/finish/pallas_call | solution.py:447
  207.7 2.6 collective-permute-start.42
  210.4 3.7 collective-permute-done.64
  218.9 4.5 collective-permute-done.33
  229.0 4.7 %collective-permute-done.43 = bf16[48,768]{1,0:T(8,128)(2,1)S(1)} collective-permute-done((bf16[48,768]{1,0:T(8,128)(2,1)S(1)}, bf16[48,768]{1,0:T(8,128)(2,1)S(1)}, u32[]{:S(2)}, u32[]{:S(2)}) %collective-permute-start.43) | collective-permute-done | bytes 73760 | tf_op jit(solution)/shard_map/ppermute | solution.py:677
  249.9 45.2 %attend_back.1 = (f32[1024,768]{1,0:T(8,128)}, f32[3,768]{1,0:T(4,128)}, bf16[768,1536]{1,0:T(8,128)(2,1)}, f32[3,9,384]{2,1,0:T(8,128)}, f32[1024,768]{1,0:T(8,128)}) custom-call(s32[8]{0:T(128)} %stack.45.sc, f32[1024,768]{1,0:T(8,128)} %get-tuple-element.53.normed_grad, bf16[1024,768]{1,0:T(8,128)(2,1)} %collective-permute-done.10.normed_grad_other, ...), custom_call_target="tpu_custom_call" | custom-call | flops 8000000000 | bytes 30000000 | tf_op jit(solution)/shard_map/attend_back/pallas_call | solution.py:577
  295.1 2.8 broadcast_select_fusion.12
  308.2 15.5 %collective-permute-done.16 = bf16[384,1536]{1,0:T(8,128)(2,1)S(1)} collective-permute-done((bf16[384,1536]{1,0:T(8,128)(2,1)}, bf16[384,1536]{1,0:T(8,128)(2,1)S(1)}, u32[]{:S(2)}, u32[]{:S(2)}) %collective-permute-start.16) | collective-permute-done | bytes 1179680 | tf_op jit(solution)/shard_map/ppermute | solution.py:677
  330.0 6.4 %collective-permute-done.17 = bf16[192,1536]{1,0:T(8,128)(2,1)S(1)} collective-permute-done((bf16[192,1536]{1,0:T(8,128)(2,1)S(1)}, bf16[192,1536]{1,0:T(8,128)(2,1)S(1)}, u32[]{:S(2)}, u32[]{:S(2)}) %collective-permute-start.17) | collective-permute-done | bytes 589856 | tf_op jit(solution)/shard_map/ppermute | solution.py:677
  339.7 4.7 %collective-permute-done.27 = f32[9,3,384]{2,1,0:T(4,128)S(1)} collective-permute-done((f32[9,3,384]{2,1,0:T(4,128)S(1)}, f32[9,3,384]{2,1,0:T(4,128)S(1)}, u32[]{:S(2)}, u32[]{:S(2)}) %collective-permute-start.27) | collective-permute-done | bytes 41504 | tf_op jit(solution)/shard_map/ppermute | solution.py:677
  347.2 8.8 %collective-permute-done.28 = f32[9,3,384]{2,1,0:T(4,128)S(1)} collective-permute-done((f32[9,3,384]{2,1,0:T(4,128)S(1)}, f32[9,3,384]{2,1,0:T(4,128)S(1)}, u32[]{:S(2)}, u32[]{:S(2)}) %collective-permute-start.28) | collective-permute-done | bytes 41504 | tf_op jit(solution)/shard_map/ppermute | solution.py:677
  359.5 8.1 %collective-permute-done.19 = bf16[48,1536]{1,0:T(8,128)(2,1)S(1)} collective-permute-done((bf16[48,1536]{1,0:T(8,128)(2,1)S(1)}, bf16[48,1536]{1,0:T(8,128)(2,1)S(1)}, u32[]{:S(2)}, u32[]{:S(2)}) %collective-permute-start.19) | collective-permute-done | bytes 147488 | tf_op jit(solution)/shard_map/ppermute | solution.py:677
  370.7 7.2 %collective-permute-done.20 = bf16[48,1536]{1,0:T(8,128)(2,1)S(1)} collective-permute-done((bf16[48,1536]{1,0:T(8,128)(2,1)S(1)}, bf16[48,1536]{1,0:T(8,128)(2,1)S(1)}, u32[]{:S(2)}, u32[]{:S(2)}) %collective-permute-start.20) | collective-permute-done | bytes 147488 | tf_op jit(solution)/shard_map/ppermute | solution.py:677
  379.4 7.6 %collective-permute-done.21 = bf16[96,1536]{1,0:T(8,128)(2,1)S(1)} collective-permute-done((bf16[96,1536]{1,0:T(8,128)(2,1)S(1)}, bf16[96,1536]{1,0:T(8,128)(2,1)S(1)}, u32[]{:S(2)}, u32[]{:S(2)}) %collective-permute-start.21) | collective-permute-done | bytes 294944 | tf_op jit(solution)/shard_map/ppermute | solution.py:677
  390.8 6.4 %input_grad.1 = (bf16[256,768]{1,0:T(8,128)(2,1)}, bf16[256,768]{1,0:T(8,128)(2,1)}, f32[2,768]{1,0:T(2,128)}) custom-call(s32[8]{0:T(128)} %stack.45.sc, f32[8,2,64,768]{3,2,1,0:T(8,128)} %bitcast.56, bf16[8,64,768]{2,1,0:T(8,128)(2,1)} %collective-permute-done.11.grad_other, f32[8,2,64,768]{3,2,1,0:T(8,128)} %bitcast.59, bf16[8,2,64,768]{3,2,1,0:T(8,128)(2,1)} %bitcast.60, ...), custom_call_target="tpu_custom_call" | custom-call | flops 300000000 | bytes 6000000 | tf_op jit(solution)/shard_map/input_grad/pallas_call | solution.py:656
  398.5 3.7 collective-permute-start.13
  410.0 30.8 %collective-permute-done.15 = f32[6,768]{1,0:T(8,128)S(1)} collective-permute-done((f32[6,768]{1,0:T(8,128)S(1)}, f32[6,768]{1,0:T(8,128)S(1)}, u32[]{:S(2)}, u32[]{:S(2)}) %collective-permute-start.15) | collective-permute-done | bytes 18464 | tf_op jit(solution)/shard_map/ppermute | solution.py:677
  448.9 4.3 maximum_convert_fusion
  453.3 4.0 maximum_convert_fusion.1
  458.9 3.5 convert_element_type.230
  (339 shorter events, 133.4 us)
Async XLA Ops:
  5.0 17.4 %collective-permute-start.1 = (bf16[256,768]{1,0:T(8,128)(2,1)S(1)}, bf16[256,768]{1,0:T(8,128)(2,1)S(1)}, u32[]{:S(2)}, u32[]{:S(2)}) collective-permute-start(bf16[256,768]{1,0:T(8,128)(2,1)S(1)} %get-tuple-element.107.p0), channel_id=1, source_target_pairs={{0,1},{1,0},{2,3},{3,2},{4,5},{5,4},{6,7},{7,6},{8,9},{9,8},{10,11... | collective-permute-start | bytes 1179656 | tf_op jit(solution)/shard_map/ppermute | solution.py:677
  5.0 16.7 %collective-permute-start.3 = (bf16[1,4608]{1,0:T(2,128)(2,1)S(1)}, bf16[1,4608]{1,0:T(2,128)(2,1)S(1)}, u32[]{:S(2)}, u32[]{:S(2)}) collective-permute-start(bf16[1,4608]{1,0:T(2,128)(2,1)S(1)} %copy-done.33), channel_id=1, source_target_pairs={{4,0},{8,4},{12,8},{16,12},{20,16},{24,20},{28,24},{5,1},{9,5},{13... | collective-permute-start | bytes 27656 | tf_op jit(solution)/shard_map/ppermute | solution.py:741
  14.2 35.1 %collective-permute-start.5 = (bf16[256,768]{1,0:T(8,128)(2,1)S(1)}, bf16[256,768]{1,0:T(8,128)(2,1)}, u32[]{:S(2)}, u32[]{:S(2)}) collective-permute-start(bf16[256,768]{1,0:T(8,128)(2,1)S(1)} %get-tuple-element.104), channel_id=1, source_target_pairs={{0,2},{1,3},{2,0},{3,1},{4,6},{5,7},{6,4},{7,5},{8,10},{9,11},{10,... | collective-permute-start | bytes 1179656 | tf_op jit(solution)/shard_map/ppermute | solution.py:677
  124.6 66.7 %collective-permute-start.8 = (bf16[8,64,768]{2,1,0:T(8,128)(2,1)}, bf16[8,64,768]{2,1,0:T(8,128)(2,1)}, u32[]{:S(2)}, u32[]{:S(2)}) collective-permute-start(bf16[8,64,768]{2,1,0:T(8,128)(2,1)} %fusion), channel_id=1, source_target_pairs={{0,1},{1,0},{2,3},{3,2},{4,5},{5,4},{6,7},{7,6},{8,9},{9,8},{10,11... | collective-permute-start | bytes 2359304 | tf_op jit(solution)/shard_map/ppermute | solution.py:677
  127.9 121.9 %collective-permute-start.10 = (bf16[1024,768]{1,0:T(8,128)(2,1)}, bf16[1024,768]{1,0:T(8,128)(2,1)}, u32[]{:S(2)}, u32[]{:S(2)}) collective-permute-start(bf16[1024,768]{1,0:T(8,128)(2,1)} %convert_element_type.215), channel_id=1, source_target_pairs={{0,1},{1,0},{2,3},{3,2},{4,5},{5,4},{6,7},{7,6},{8,9},{9,8},{10,11... | collective-permute-start | bytes 4718600 | tf_op jit(solution)/shard_map/ppermute | solution.py:677
  131.0 32.6 %collective-permute-start.39 = (bf16[384,768]{1,0:T(8,128)(2,1)}, bf16[384,768]{1,0:T(8,128)(2,1)S(1)}, u32[]{:S(2)}, u32[]{:S(2)}) collective-permute-start(bf16[384,768]{1,0:T(8,128)(2,1)} %broadcast_select_fusion.21), channel_id=1, source_target_pairs={{0,2},{1,3},{2,0},{3,1},{4,6},{5,7},{6,4},{7,5},{8,10},{9,11},{10,... | collective-permute-start | bytes 1769480 | tf_op jit(solution)/shard_map/ppermute | solution.py:677
  136.8 30.5 %collective-permute-start.30 = (bf16[384,768]{1,0:T(8,128)(2,1)}, bf16[384,768]{1,0:T(8,128)(2,1)}, u32[]{:S(2)}, u32[]{:S(2)}) collective-permute-start(bf16[384,768]{1,0:T(8,128)(2,1)} %broadcast_select_fusion.24), channel_id=1, source_target_pairs={{0,2},{1,3},{2,0},{3,1},{4,6},{5,7},{6,4},{7,5},{8,10},{9,11},{10,... | collective-permute-start | bytes 1769480 | tf_op jit(solution)/shard_map/ppermute | solution.py:677
  140.2 20.7 %collective-permute-start.51 = (f32[9,1536]{1,0:T(8,128)S(1)}, f32[9,1536]{1,0:T(8,128)S(1)}, u32[]{:S(2)}, u32[]{:S(2)}) collective-permute-start(f32[9,1536]{1,0:T(8,128)S(1)} %add.168), channel_id=1, source_target_pairs={{0,2},{1,3},{2,0},{3,1},{4,6},{5,7},{6,4},{7,5},{8,10},{9,11},{10,... | collective-permute-start | bytes 165896 | tf_op jit(solution)/shard_map/ppermute | solution.py:677
  162.3 16.5 %collective-permute-start.62 = (bf16[384,768]{1,0:T(8,128)(2,1)}, bf16[384,768]{1,0:T(8,128)(2,1)}, u32[]{:S(2)}, u32[]{:S(2)}) collective-permute-start(bf16[384,768]{1,0:T(8,128)(2,1)} %broadcast_select_fusion.15), channel_id=1, source_target_pairs={{0,2},{1,3},{2,0},{3,1},{4,6},{5,7},{6,4},{7,5},{8,10},{9,11},{10,... | collective-permute-start | bytes 1769480 | tf_op jit(solution)/shard_map/ppermute | solution.py:677
  163.6 26.9 %collective-permute-start.53 = (bf16[384,768]{1,0:T(8,128)(2,1)}, bf16[384,768]{1,0:T(8,128)(2,1)S(1)}, u32[]{:S(2)}, u32[]{:S(2)}) collective-permute-start(bf16[384,768]{1,0:T(8,128)(2,1)} %broadcast_select_fusion.18), channel_id=1, source_target_pairs={{0,2},{1,3},{2,0},{3,1},{4,6},{5,7},{6,4},{7,5},{8,10},{9,11},{10,... | collective-permute-start | bytes 1769480 | tf_op jit(solution)/shard_map/ppermute | solution.py:677
  167.3 30.6 %collective-permute-start.40 = (bf16[192,768]{1,0:T(8,128)(2,1)}, bf16[192,768]{1,0:T(8,128)(2,1)}, u32[]{:S(2)}, u32[]{:S(2)}) collective-permute-start(bf16[192,768]{1,0:T(8,128)(2,1)} %broadcast_select_fusion.40), channel_id=1, source_target_pairs={{0,4},{4,0},{8,12},{12,8},{16,20},{20,16},{24,28},{28,24},{1,5},{5... | collective-permute-start | bytes 884744 | tf_op jit(solution)/shard_map/ppermute | solution.py:677
  178.8 20.8 %collective-permute-start.31 = (bf16[192,768]{1,0:T(8,128)(2,1)}, bf16[192,768]{1,0:T(8,128)(2,1)}, u32[]{:S(2)}, u32[]{:S(2)}) collective-permute-start(bf16[192,768]{1,0:T(8,128)(2,1)} %broadcast_select_fusion.43), channel_id=1, source_target_pairs={{0,4},{4,0},{8,12},{12,8},{16,20},{20,16},{24,28},{28,24},{1,5},{5... | collective-permute-start | bytes 884744 | tf_op jit(solution)/shard_map/ppermute | solution.py:677
  197.9 41.9 %collective-permute-start.9 = (bf16[256,768]{1,0:T(8,128)(2,1)}, bf16[256,768]{1,0:T(8,128)(2,1)S(1)}, u32[]{:S(2)}, u32[]{:S(2)}) collective-permute-start(bf16[256,768]{1,0:T(8,128)(2,1)} %get-tuple-element.52), channel_id=1, source_target_pairs={{0,2},{1,3},{2,0},{3,1},{4,6},{5,7},{6,4},{7,5},{8,10},{9,11},{10,... | collective-permute-start | bytes 1179656 | tf_op jit(solution)/shard_map/ppermute | solution.py:677
  239.8 58.7 %collective-permute-start.58 = (bf16[96,768]{1,0:T(8,128)(2,1)S(1)}, bf16[96,768]{1,0:T(8,128)(2,1)}, u32[]{:S(2)}, u32[]{:S(2)}) collective-permute-start(bf16[96,768]{1,0:T(8,128)(2,1)S(1)} %pad_maximum_fusion.21), channel_id=1, source_target_pairs={{0,8},{4,12},{8,0},{12,4},{16,24},{20,28},{24,16},{28,20},{1,9},{5... | collective-permute-start | bytes 442376 | tf_op jit(solution)/shard_map/ppermute | solution.py:677
  242.3 64.1 %collective-permute-start.45 = (bf16[192,768]{1,0:T(8,128)(2,1)S(1)}, bf16[192,768]{1,0:T(8,128)(2,1)S(1)}, u32[]{:S(2)}, u32[]{:S(2)}) collective-permute-start(bf16[192,768]{1,0:T(8,128)(2,1)S(1)} %pad_maximum_fusion.15), channel_id=1, source_target_pairs={{0,4},{4,0},{8,12},{12,8},{16,20},{20,16},{24,28},{28,24},{1,5},{5... | collective-permute-start | bytes 884744 | tf_op jit(solution)/shard_map/ppermute | solution.py:677
  246.2 78.0 %collective-permute-start.36 = (bf16[192,768]{1,0:T(8,128)(2,1)}, bf16[192,768]{1,0:T(8,128)(2,1)}, u32[]{:S(2)}, u32[]{:S(2)}) collective-permute-start(bf16[192,768]{1,0:T(8,128)(2,1)} %pad_maximum_fusion.14), channel_id=1, source_target_pairs={{0,4},{4,0},{8,12},{12,8},{16,20},{20,16},{24,28},{28,24},{1,5},{5... | collective-permute-start | bytes 884744 | tf_op jit(solution)/shard_map/ppermute | solution.py:677
  249.4 79.3 %collective-permute-start.68 = (bf16[192,768]{1,0:T(8,128)(2,1)}, bf16[192,768]{1,0:T(8,128)(2,1)}, u32[]{:S(2)}, u32[]{:S(2)}) collective-permute-start(bf16[192,768]{1,0:T(8,128)(2,1)} %pad_maximum_fusion.17), channel_id=1, source_target_pairs={{0,4},{4,0},{8,12},{12,8},{16,20},{20,16},{24,28},{28,24},{1,5},{5... | collective-permute-start | bytes 884744 | tf_op jit(solution)/shard_map/ppermute | solution.py:677
  297.9 25.9 %collective-permute-start.16 = (bf16[384,1536]{1,0:T(8,128)(2,1)}, bf16[384,1536]{1,0:T(8,128)(2,1)S(1)}, u32[]{:S(2)}, u32[]{:S(2)}) collective-permute-start(bf16[384,1536]{1,0:T(8,128)(2,1)} %broadcast_select_fusion.12), channel_id=1, source_target_pairs={{0,2},{1,3},{2,0},{3,1},{4,6},{5,7},{6,4},{7,5},{8,10},{9,11},{10,... | collective-permute-start | bytes 3538952 | tf_op jit(solution)/shard_map/ppermute | solution.py:677
  304.7 32.0 %collective-permute-start.59 = (bf16[192,768]{1,0:T(8,128)(2,1)}, bf16[192,768]{1,0:T(8,128)(2,1)S(1)}, u32[]{:S(2)}, u32[]{:S(2)}) collective-permute-start(bf16[192,768]{1,0:T(8,128)(2,1)} %pad_maximum_fusion.16), channel_id=1, source_target_pairs={{0,4},{4,0},{8,12},{12,8},{16,20},{20,16},{24,28},{28,24},{1,5},{5... | collective-permute-start | bytes 884744 | tf_op jit(solution)/shard_map/ppermute | solution.py:677
  307.1 83.6 %collective-permute-start.11 = (bf16[8,64,768]{2,1,0:T(8,128)(2,1)}, bf16[8,64,768]{2,1,0:T(8,128)(2,1)}, u32[]{:S(2)}, u32[]{:S(2)}) collective-permute-start(bf16[8,64,768]{2,1,0:T(8,128)(2,1)} %fusion.1), channel_id=1, source_target_pairs={{0,1},{1,0},{2,3},{3,2},{4,5},{5,4},{6,7},{7,6},{8,9},{9,8},{10,11... | collective-permute-start | bytes 2359304 | tf_op jit(solution)/shard_map/ppermute | solution.py:677
  323.7 14.9 %collective-permute-start.26 = (f32[9,3,384]{2,1,0:T(4,128)S(1)}, f32[9,3,384]{2,1,0:T(4,128)S(1)}, u32[]{:S(2)}, u32[]{:S(2)}) collective-permute-start(f32[9,3,384]{2,1,0:T(4,128)S(1)} %fusion.4), channel_id=1, source_target_pairs={{0,8},{4,12},{8,0},{12,4},{16,24},{20,28},{24,16},{28,20},{1,9},{5... | collective-permute-start | bytes 124424 | tf_op jit(solution)/shard_map/ppermute | solution.py:677
  328.6 40.7 %collective-permute-start.46 = (bf16[384,768]{1,0:T(8,128)(2,1)}, bf16[384,768]{1,0:T(8,128)(2,1)}, u32[]{:S(2)}, u32[]{:S(2)}) collective-permute-start(bf16[384,768]{1,0:T(8,128)(2,1)} %pad_maximum_fusion.10), channel_id=1, source_target_pairs={{0,2},{1,3},{2,0},{3,1},{4,6},{5,7},{6,4},{7,5},{8,10},{9,11},{10,... | collective-permute-start | bytes 1769480 | tf_op jit(solution)/shard_map/ppermute | solution.py:677
  336.4 42.7 %collective-permute-start.37 = (bf16[384,768]{1,0:T(8,128)(2,1)}, bf16[384,768]{1,0:T(8,128)(2,1)S(1)}, u32[]{:S(2)}, u32[]{:S(2)}) collective-permute-start(bf16[384,768]{1,0:T(8,128)(2,1)} %pad_maximum_fusion.9), channel_id=1, source_target_pairs={{0,2},{1,3},{2,0},{3,1},{4,6},{5,7},{6,4},{7,5},{8,10},{9,11},{10,... | collective-permute-start | bytes 1769480 | tf_op jit(solution)/shard_map/ppermute | solution.py:677
  336.7 19.5 %collective-permute-start.18 = (bf16[96,1536]{1,0:T(8,128)(2,1)S(1)}, bf16[96,1536]{1,0:T(8,128)(2,1)S(1)}, u32[]{:S(2)}, u32[]{:S(2)}) collective-permute-start(bf16[96,1536]{1,0:T(8,128)(2,1)S(1)} %broadcast_select_fusion.46), channel_id=1, source_target_pairs={{0,8},{4,12},{8,0},{12,4},{16,24},{20,28},{24,16},{28,20},{1,9},{5... | collective-permute-start | bytes 884744 | tf_op jit(solution)/shard_map/ppermute | solution.py:677
  356.0 33.4 %collective-permute-start.69 = (bf16[384,768]{1,0:T(8,128)(2,1)}, bf16[384,768]{1,0:T(8,128)(2,1)}, u32[]{:S(2)}, u32[]{:S(2)}) collective-permute-start(bf16[384,768]{1,0:T(8,128)(2,1)} %pad_maximum_fusion.12), channel_id=1, source_target_pairs={{0,2},{1,3},{2,0},{3,1},{4,6},{5,7},{6,4},{7,5},{8,10},{9,11},{10,... | collective-permute-start | bytes 1769480 | tf_op jit(solution)/shard_map/ppermute | solution.py:677
  367.5 37.1 %collective-permute-start.60 = (bf16[384,768]{1,0:T(8,128)(2,1)}, bf16[384,768]{1,0:T(8,128)(2,1)}, u32[]{:S(2)}, u32[]{:S(2)}) collective-permute-start(bf16[384,768]{1,0:T(8,128)(2,1)} %pad_maximum_fusion.11), channel_id=1, source_target_pairs={{0,2},{1,3},{2,0},{3,1},{4,6},{5,7},{6,4},{7,5},{8,10},{9,11},{10,... | collective-permute-start | bytes 1769480 | tf_op jit(solution)/shard_map/ppermute | solution.py:677
  379.1 65.4 %collective-permute-start.47 = (bf16[768,768]{1,0:T(8,128)(2,1)}, bf16[768,768]{1,0:T(8,128)(2,1)}, u32[]{:S(2)}, u32[]{:S(2)}) collective-permute-start(bf16[768,768]{1,0:T(8,128)(2,1)} %pad_maximum_fusion.3), channel_id=1, source_target_pairs={{0,1},{1,0},{2,3},{3,2},{4,5},{5,4},{6,7},{7,6},{8,9},{9,8},{10,11... | collective-permute-start | bytes 3538952 | tf_op jit(solution)/shard_map/ppermute | solution.py:677
  388.0 14.7 %collective-permute-start.22 = (bf16[192,1536]{1,0:T(8,128)(2,1)}, bf16[192,1536]{1,0:T(8,128)(2,1)}, u32[]{:S(2)}, u32[]{:S(2)}) collective-permute-start(bf16[192,1536]{1,0:T(8,128)(2,1)} %pad_maximum_fusion.8), channel_id=1, source_target_pairs={{0,4},{4,0},{8,12},{12,8},{16,20},{20,16},{24,28},{28,24},{1,5},{5... | collective-permute-start | bytes 1769480 | tf_op jit(solution)/shard_map/ppermute | solution.py:677
  389.3 56.9 %collective-permute-start.38 = (bf16[768,768]{1,0:T(8,128)(2,1)}, bf16[768,768]{1,0:T(8,128)(2,1)}, u32[]{:S(2)}, u32[]{:S(2)}) collective-permute-start(bf16[768,768]{1,0:T(8,128)(2,1)} %pad_maximum_fusion.2), channel_id=1, source_target_pairs={{0,1},{1,0},{2,3},{3,2},{4,5},{5,4},{6,7},{7,6},{8,9},{9,8},{10,11... | collective-permute-start | bytes 3538952 | tf_op jit(solution)/shard_map/ppermute | solution.py:677
  404.3 39.6 %collective-permute-start.23 = (bf16[384,1536]{1,0:T(8,128)(2,1)S(1)}, bf16[384,1536]{1,0:T(8,128)(2,1)S(1)}, u32[]{:S(2)}, u32[]{:S(2)}) collective-permute-start(bf16[384,1536]{1,0:T(8,128)(2,1)S(1)} %pad_maximum_fusion.1), channel_id=1, source_target_pairs={{0,2},{1,3},{2,0},{3,1},{4,6},{5,7},{6,4},{7,5},{8,10},{9,11},{10,... | collective-permute-start | bytes 3538952 | tf_op jit(solution)/shard_map/ppermute | solution.py:677
  406.5 35.5 %collective-permute-start.12 = (bf16[256,768]{1,0:T(8,128)(2,1)S(1)}, bf16[256,768]{1,0:T(8,128)(2,1)S(1)}, u32[]{:S(2)}, u32[]{:S(2)}) collective-permute-start(bf16[256,768]{1,0:T(8,128)(2,1)S(1)} %copy-done.37), channel_id=1, source_target_pairs={{0,2},{1,3},{2,0},{3,1},{4,6},{5,7},{6,4},{7,5},{8,10},{9,11},{10,... | collective-permute-start | bytes 1179656 | tf_op jit(solution)/shard_map/ppermute | solution.py:677
  409.0 31.7 %collective-permute-start.15 = (f32[6,768]{1,0:T(8,128)S(1)}, f32[6,768]{1,0:T(8,128)S(1)}, u32[]{:S(2)}, u32[]{:S(2)}) collective-permute-start(f32[6,768]{1,0:T(8,128)S(1)} %add.148), channel_id=1, source_target_pairs={{0,2},{1,3},{2,0},{3,1},{4,6},{5,7},{6,4},{7,5},{8,10},{9,11},{10,... | collective-permute-start | bytes 55304 | tf_op jit(solution)/shard_map/ppermute | solution.py:677
  (80 other events, 718.7 us)

commit v2 on v1

--- a/solution.py
+++ b/solution.py
@@ -26,6 +26,13 @@
     return lax.dot_general(
         left, right, (((left_dim,), (right_dim,)), ((), ())), preferred_element_type=F32
     )
+
+
+ANYWHERE = pl.BlockSpec(memory_space=pl.ANY)
+
+
+def full(*shape):
+    return pl.BlockSpec(shape, lambda i, s: (0,) * len(shape))
 
 
 def iota(shape, dim):
@@ -274,7 +281,6 @@
 
 
 def project_out(sc, mixed_own, mixed_other, base, out_weight, mod, pieces):
-    full = lambda *shape: pl.BlockSpec(shape, lambda i, s: (0,) * len(shape))
     tokens = full(1024, 768)
     return pl.pallas_call(
         middle_kernel,
@@ -299,17 +305,25 @@
     )(sc, mixed_own, mixed_other, base, out_weight, mod, *pieces)
 
 
-BLOCK = 256
-
-
-def feed_kernel(
-    first, sc, normed, branch_grad, up, down, kernel, *rest,
-):
+BLOCK = 384
+
+
+def split_halves(core, g, values, keep, send):
+    for local in range(2):
+        low = values[128 * local : 128 * local + 64, :]
+        high = values[128 * local + 64 : 128 * local + 128, :]
+        keep[2 * g + local] = jnp.where(core == 0, low, high)
+        send[2 * g + local] = jnp.where(core == 0, high, low).astype(BF)
+
+
+def feed_kernel(count, first, sc, normed, branch_grad, up, down, kernel, *rest):
+    rest = rest[count:]
     if first:
-        (down_grad, up_grad, kernel_grad, branch_out, normed_grad_out,
+        (up_keep, up_send, down_keep, down_send, kernel_grad, branch_out, normed_grad_out,
          held, normed_t, hid, d_act, acts, d_conv, d_hids) = rest
     else:
-        (branch_in, normed_grad_in, down_grad, up_grad, kernel_grad, branch_out, normed_grad_out,
+        (branch_in, normed_grad_in, up_keep, up_send, down_keep, down_send, kernel_grad,
+         branch_keep, branch_send, normed_grad_out, normed_grad_send,
          held, normed_t, hid, d_act, acts, d_conv, d_hids) = rest
     step = pl.program_id(0)
 
@@ -348,46 +362,56 @@
             d_hids[pl.ds(g * 256 + start, STEP), dest] = total.astype(BF)
 
         kernel_grad[:, cols] = convolve_back(held, weights, source, write)
-    down_grad[block, :] = dot(acts[:, block].T, branch_grad[...]).astype(BF)
-    up_grad[:, block] = dot(normed_t[...], d_hids[:, block]).astype(BF)
+    grad = dot(acts[:, block].T, branch_grad[...]).astype(BF)
+
+    @pl.when(step == sc[8])
+    def _():
+        down_keep[...] = grad
+
+    @pl.when(step != sc[8])
+    def _():
+        down_send[...] = grad
 
     @pl.when(step == pl.num_programs(0) - 1)
     def _():
-        for r in range(0, 1024, 512):
-            rows = slice(r, r + 512)
+        for pair, out in ((sc[7], up_keep), (1 - sc[7], up_send)):
+            rows = pl.ds(pl.multiple_of(pair * 384, 384), 384)
+            out[...] = dot(normed_t[rows, :], d_hids[...]).astype(BF)
+        for r in range(0, 1024, 256):
+            rows = slice(r, r + 256)
             branch = dot(acts[rows, :], down[...])
             normed_grad = dot(d_hids[rows, :], up[...], 1, 1)
-            if not first:
-                branch = branch + branch_in[rows, :]
+            if first:
+                branch_out[rows, :] = branch
+                normed_grad_out[rows, :] = normed_grad
+            else:
+                split_halves(sc[6], r // 256, branch + branch_in[rows, :], branch_keep, branch_send)
                 normed_grad = normed_grad + normed_grad_in[rows, :]
-            branch_out[rows, :] = branch
-            normed_grad_out[rows, :] = normed_grad
-
-
-def feed(sc, normed, branch_grad, up_weight, down_weight, ffn_kernel, half, before):
-    full = lambda *shape: pl.BlockSpec(shape, lambda i, s: (0,) * len(shape))
+                normed_grad_out[rows, :] = normed_grad
+                normed_grad_send[rows, :] = normed_grad.astype(BF)
+
+
+def feed(sc, normed, branch_grad, up_weight, down_weight, ffn_kernel, half, before, deps=()):
     tokens = full(1024, 768)
     first = before is None
+    piece = jax.ShapeDtypeStruct((384, 768), BF)
     return pl.pallas_call(
-        functools.partial(feed_kernel, first),
+        functools.partial(feed_kernel, len(deps), first),
         grid_spec=pltpu.PrefetchScalarGridSpec(
             num_scalar_prefetch=1,
-            grid=(3,),
+            grid=(2,),
             in_specs=[
                 tokens,
                 tokens,
                 pl.BlockSpec((768, 768), lambda i, s: (0, 2 * s[6] + half)),
                 pl.BlockSpec((768, 768), lambda i, s: (2 * s[6] + half, 0)),
-                pl.BlockSpec((9, BLOCK), lambda i, s: (0, 6 * s[6] + 3 * half + i)),
+                pl.BlockSpec((9, BLOCK), lambda i, s: (0, 4 * s[6] + 2 * half + i)),
             ]
+            + [ANYWHERE] * len(deps)
             + ([] if first else [tokens, tokens]),
-            out_specs=[
-                full(768, 768),
-                full(768, 768),
-                pl.BlockSpec((9, BLOCK), lambda i, s: (0, i)),
-                tokens,
-                tokens,
-            ],
+            out_specs=[full(384, 768)] * 4
+            + [pl.BlockSpec((9, BLOCK), lambda i, s: (0, i))]
+            + ([tokens, tokens] if first else [full(8, 64, 768), full(8, 64, 768), tokens, tokens]),
             scratch_shapes=[
                 pltpu.VMEM((2 * GROUPS, 2 * MARGIN + 256, LANES), F32),
                 pltpu.VMEM((768, 1024), BF),
@@ -398,20 +422,25 @@
                 pltpu.VMEM((1024, 768), BF),
             ],
         ),
-        out_shape=[
-            jax.ShapeDtypeStruct((768, 768), BF),
-            jax.ShapeDtypeStruct((768, 768), BF),
-            jax.ShapeDtypeStruct((9, 768), F32),
+        out_shape=[piece] * 4
+        + [jax.ShapeDtypeStruct((9, 768), F32)]
+        + (
+            []
+            if first
+            else [jax.ShapeDtypeStruct((8, 64, 768), F32), jax.ShapeDtypeStruct((8, 64, 768), BF)]
+        )
+        + [
             jax.ShapeDtypeStruct((1024, 768), F32),
-            jax.ShapeDtypeStruct((1024, 768), F32),
+            jax.ShapeDtypeStruct((1024, 768), F32 if first else BF),
         ],
         compiler_params=pltpu.CompilerParams(vmem_limit_bytes=VMEM_LIMIT),
-        cost_estimate=pl.CostEstimate(flops=7_500_000_000, bytes_accessed=20_000_000, transcendentals=800000),
+        cost_estimate=pl.CostEstimate(flops=15_000_000_000, bytes_accessed=60_000_000, transcendentals=800000),
         name="feed",
-    )(sc, normed, branch_grad, up_weight, down_weight, ffn_kernel, *([] if first else before))
-
-
-def finish_kernel(sc, middle, branch, branch_other, seed, mod, near_out, far_out, sums_out):
+    )(sc, normed, branch_grad, up_weight, down_weight, ffn_kernel, *deps, *([] if first else before))
+
+
+def finish_kernel(count, sc, middle, branch, branch_other, seed, mod, *rest):
+    near_out, far_out, sums_out = rest[count:]
     height, breadth, core = sc[0], sc[1], sc[6]
     gate, factor = mod[5:6, :], mod[6:7, :]
     matrix = to_phase_matrix()
@@ -420,7 +449,7 @@
         parts = []
         for g in range(GROUPS):
             token = phase_rows(64, g * 256 + (2 * local + core) * 64)
-            whole = branch[2 * g + local, 0] + branch_other[2 * g + local].astype(F32)
+            whole = branch[2 * g + local] + branch_other[2 * g + local].astype(F32)
             total = total + col_sum(seed[2 * g + local, 0].astype(F32) * whole)
             result = middle[2 * g + local, 0] + gate * whole
             parts.append((result * live_rows(token, height, breadth)).astype(BF))
@@ -441,15 +470,15 @@
     return pl.BlockSpec((8, 1, 64, 768), lambda i, s: (0, s[6], 0, 0))
 
 
-def finish(sc, middle, branch, branch_other, seed, mod):
-    full = lambda *shape: pl.BlockSpec(shape, lambda i, s: (0,) * len(shape))
+def finish(sc, middle, branch, branch_other, seed, mod, deps=()):
     halves = lambda v: v.reshape(8, 2, 64, 768)
     return pl.pallas_call(
-        finish_kernel,
+        functools.partial(finish_kernel, len(deps)),
         grid_spec=pltpu.PrefetchScalarGridSpec(
             num_scalar_prefetch=1,
             grid=(1,),
-            in_specs=[half_spec(), half_spec(), full(8, 64, 768), half_spec(), full(8, 768)],
+            in_specs=[half_spec(), full(8, 64, 768), full(8, 64, 768), half_spec(), full(8, 768)]
+            + [ANYWHERE] * len(deps),
             out_specs=[full(256, 768), full(256, 768), full(1, 768)],
         ),
         out_shape=[
@@ -460,52 +489,74 @@
         compiler_params=pltpu.CompilerParams(vmem_limit_bytes=VMEM_LIMIT),
         cost_estimate=pl.CostEstimate(flops=300_000_000, bytes_accessed=6_000_000, transcendentals=0),
         name="finish",
-    )(sc, halves(middle), halves(branch), branch_other, halves(seed), mod)
+    )(sc, halves(middle), branch, branch_other, halves(seed), mod, *deps)
+
+
+def norm_back_kernel(
+    count, sc, normed_grad, normed_grad_other, middle, attended, seed, mod, mixed, *rest,
+):
+    middle_grad, att_grad, sums_out, out_keep, out_send = rest[count:]
+    gate, scale, factor = mod[2:3, :], 1.0 + mod[4:5, :], mod[6:7, :]
+
+    def at(i, sums):
+        d_shift, d_scale, d_gate = sums
+        rows = pl.ds(pl.multiple_of(i * 64, 64), 64)
+        grad = normed_grad[rows, :] + normed_grad_other[rows, :].astype(F32)
+        unit, inverse = normal(middle[rows, :])
+        both = grad * unit
+        d_shift = d_shift + col_sum(grad)
+        d_scale = d_scale + col_sum(both)
+        grad = grad * scale
+        mean = jnp.mean(grad, axis=-1, keepdims=True)
+        along = jnp.mean(both * scale, axis=-1, keepdims=True)
+        total = seed[rows, :].astype(F32) * factor + inverse * (grad - mean - unit * along)
+        middle_grad[rows, :] = total
+        d_gate = d_gate + col_sum(total * attended[rows, :].astype(F32))
+        att_grad[rows, :] = (total * gate).astype(BF)
+        return d_shift, d_scale, d_gate
+
+    zero = jnp.zeros((1, 768), F32)
+    sums = lax.fori_loop(0, 16, at, (zero, zero, zero))
+    for k in range(3):
+        sums_out[k : k + 1, :] = 0.5 * sums[k]
+    mixed_t = mixed[...].T
+    for at_y, out in ((sc[8], out_keep), (1 - sc[8], out_send)):
+        cols = pl.ds(pl.multiple_of(at_y * 384, 384), 384)
+        out[...] = dot(mixed_t, att_grad[:, cols]).astype(BF)
+
+
+def norm_back(sc, normed_grad, normed_grad_other, middle, attended, seed, mod, mixed, deps=()):
+    tokens = full(1024, 768)
+    return pl.pallas_call(
+        functools.partial(norm_back_kernel, len(deps)),
+        grid_spec=pltpu.PrefetchScalarGridSpec(
+            num_scalar_prefetch=1,
+            grid=(1,),
+            in_specs=[tokens] * 5 + [full(8, 768), full(1024, 384)] + [ANYWHERE] * len(deps),
+            out_specs=[tokens, tokens, full(3, 768), full(384, 384), full(384, 384)],
+        ),
+        out_shape=[
+            jax.ShapeDtypeStruct((1024, 768), F32),
+            jax.ShapeDtypeStruct((1024, 768), BF),
+            jax.ShapeDtypeStruct((3, 768), F32),
+            jax.ShapeDtypeStruct((384, 384), BF),
+            jax.ShapeDtypeStruct((384, 384), BF),
+        ],
+        compiler_params=pltpu.CompilerParams(vmem_limit_bytes=VMEM_LIMIT),
+        cost_estimate=pl.CostEstimate(flops=4_000_000_000, bytes_accessed=30_000_000, transcendentals=0),
+        name="norm_back",
+    )(sc, normed_grad, normed_grad_other, middle, attended, seed, mod, mixed, *deps)
 
 
 def attend_back_kernel(
-    sc, normed_grad, normed_grad_other, middle, attended, seed, mod,
-    mixed, out_weight, normed, qkv, conv, prob, wq, wk, wv, kq, kk, kv,
-    middle_grad, sums_out, weight_grad, kernel_grad, normed_grad_out,
-    held, normed_t, d_att, d_mixed, d_conv, d_qkv,
+    count, axis, sc, att_grad, out_weight, normed, qkv, conv, prob, kq, kk, kv, *rest,
 ):
-    step = pl.program_id(0)
-
-    @pl.when(step == 0)
-    def _():
-        clear_margins(held)
-        for r in range(0, 1024, 256):
-            normed_t[:, r : r + 256] = normed[r : r + 256, :].T
-        gate, scale, factor = mod[2:3, :], 1.0 + mod[4:5, :], mod[6:7, :]
-
-        def at(i, sums):
-            d_shift, d_scale, d_gate = sums
-            rows = pl.ds(pl.multiple_of(i * 64, 64), 64)
-            grad = normed_grad[rows, :] + normed_grad_other[rows, :].astype(F32)
-            unit, inverse = normal(middle[rows, :])
-            both = grad * unit
-            d_shift = d_shift + col_sum(grad)
-            d_scale = d_scale + col_sum(both)
-            grad = grad * scale
-            mean = jnp.mean(grad, axis=-1, keepdims=True)
-            along = jnp.mean(both * scale, axis=-1, keepdims=True)
-            total = seed[rows, :].astype(F32) * factor + inverse * (grad - mean - unit * along)
-            middle_grad[rows, :] = total
-            d_gate = d_gate + col_sum(total * attended[rows, :].astype(F32))
-            d_att[rows, :] = (total * gate).astype(BF)
-            return d_shift, d_scale, d_gate
-
-        zero = jnp.zeros((1, 768), F32)
-        sums = lax.fori_loop(0, 16, at, (zero, zero, zero))
-        for k in range(3):
-            sums_out[k : k + 1, :] = 0.5 * sums[k]
-        mixed_t = mixed[...].T
-        grad = dot(mixed_t, d_att[...]).astype(BF)
-        weight_grad[0:384, 1152:1536] = grad[:, 0:384]
-        weight_grad[384:768, 1152:1536] = grad[:, 384:768]
-
+    (qkv_grad, kernel_grad, weight_keep, weight_send, held, normed_t, d_mixed, d_conv) = rest[count:]
+    clear_margins(held)
+    for r in range(0, 1024, 256):
+        normed_t[:, r : r + 256] = normed[r : r + 256, :].T
     for r in range(0, 1024, 512):
-        d_mixed[r : r + 512, :] = dot(d_att[r : r + 512, :], out_weight[...], 1, 1).astype(BF)
+        d_mixed[r : r + 512, :] = dot(att_grad[r : r + 512, :], out_weight[...], 1, 1).astype(BF)
 
     lane = iota((256, LANES), 1)
 
@@ -542,80 +593,88 @@
             return qkv[0, pl.ds(g * 256 + start, STEP), cols].astype(F32)
 
         def write(g, start, total):
-            d_qkv[pl.ds(g * 256 + start, STEP), cols] = total.astype(BF)
-
-        kernel_grad[0, :, cols] = convolve_back(held, kernel[...].astype(F32), source, write)
-    grad = dot(normed_t[...], d_qkv[...]).astype(BF)
-    for s in range(3):
-        dest = pl.ds(pl.multiple_of(s * 384 + step * LANES, LANES), LANES)
-        weight_grad[:, dest] = grad[:, s * LANES : (s + 1) * LANES]
-    weight = jnp.concatenate([wq[...], wk[...], wv[...]], axis=1)
-    for r in range(0, 1024, 512):
-        part = dot(d_qkv[r : r + 512, :], weight, 1, 1)
-
-        @pl.when(step == 0)
-        def _():
-            normed_grad_out[r : r + 512, :] = part
-
-        @pl.when(step != 0)
-        def _():
-            normed_grad_out[r : r + 512, :] += part
-
-
-def attend_back(sc, normed_grad, normed_grad_other, middle, attended, seed, mod, mixed, out_weight,
-                normed, qkv, conv, prob, qkv_weight, attn_kernel):
-    full = lambda *shape: pl.BlockSpec(shape, lambda i, s: (0,) * len(shape))
+            qkv_grad[pl.ds(g * 256 + start, STEP), cols] = total.astype(BF)
+
+        kernel_grad[:, cols] = convolve_back(held, kernel[...].astype(F32), source, write)
+    for place, out in ((sc[axis], weight_keep), (1 - sc[axis], weight_send)):
+        rows = pl.ds(pl.multiple_of(place * 384, 384), 384)
+        out[...] = dot(normed_t[rows, :], qkv_grad[...]).astype(BF)
+
+
+def attend_back(sc, heads, axis, att_grad, out_weight, normed, qkv, conv, prob, attn_kernel, deps=()):
     tokens = full(1024, 768)
 
-    def weight_spec(k):
-        return pl.BlockSpec((768, LANES), lambda i, s: (0, 6 * k + 3 * s[6] + i))
-
     def kernel_spec(k):
-        return pl.BlockSpec((9, LANES), lambda i, s: (0, 6 * k + 3 * s[6] + i))
-
-    saved = pl.BlockSpec((1, 1024, 384), lambda i, s: (i, 0, 0))
+        return pl.BlockSpec((9, LANES), lambda i, s: (0, 6 * k + 3 * s[6] + heads))
+
+    saved = pl.BlockSpec((1, 1024, 384), lambda i, s: (heads, 0, 0))
     return pl.pallas_call(
-        attend_back_kernel,
+        functools.partial(attend_back_kernel, len(deps), axis),
         grid_spec=pltpu.PrefetchScalarGridSpec(
             num_scalar_prefetch=1,
-            grid=(3,),
-            in_specs=[tokens, tokens, tokens, tokens, tokens, full(8, 768), full(1024, 384),
-                      pl.BlockSpec((LANES, 768), lambda i, s: (3 * s[6] + i, 0)),
+            grid=(1,),
+            in_specs=[tokens, pl.BlockSpec((LANES, 768), lambda i, s: (3 * s[6] + heads, 0)),
                       tokens, saved, saved,
-                      pl.BlockSpec((1, GROUPS, 2, 256, 256), lambda i, s: (i, 0, 0, 0, 0))]
-            + [weight_spec(k) for k in range(3)]
-            + [kernel_spec(k) for k in range(3)],
-            out_specs=[
-                tokens,
-                full(3, 768),
-                full(768, 1536),
-                pl.BlockSpec((1, 9, 384), lambda i, s: (i, 0, 0)),
-                tokens,
-            ],
+                      pl.BlockSpec((1, GROUPS, 2, 256, 256), lambda i, s: (heads, 0, 0, 0, 0))]
+            + [kernel_spec(k) for k in range(3)]
+            + [ANYWHERE] * len(deps),
+            out_specs=[full(1024, 384), full(9, 384), full(384, 384), full(384, 384)],
             scratch_shapes=[
                 pltpu.VMEM((2 * GROUPS, 2 * MARGIN + 256, LANES), F32),
                 pltpu.VMEM((768, 1024), BF),
-                pltpu.VMEM((1024, 768), BF),
                 pltpu.VMEM((1024, LANES), BF),
-                pltpu.VMEM((1024, 384), BF),
                 pltpu.VMEM((1024, 384), BF),
             ],
         ),
         out_shape=[
-            jax.ShapeDtypeStruct((1024, 768), F32),
-            jax.ShapeDtypeStruct((3, 768), F32),
-            jax.ShapeDtypeStruct((768, 1536), BF),
-            jax.ShapeDtypeStruct((3, 9, 384), F32),
-            jax.ShapeDtypeStruct((1024, 768), F32),
+            jax.ShapeDtypeStruct((1024, 384), BF),
+            jax.ShapeDtypeStruct((9, 384), F32),
+            jax.ShapeDtypeStruct((384, 384), BF),
+            jax.ShapeDtypeStruct((384, 384), BF),
         ],
         compiler_params=pltpu.CompilerParams(vmem_limit_bytes=VMEM_LIMIT),
-        cost_estimate=pl.CostEstimate(flops=8_000_000_000, bytes_accessed=30_000_000, transcendentals=0),
+        cost_estimate=pl.CostEstimate(flops=6_000_000_000, bytes_accessed=30_000_000, transcendentals=0),
         name="attend_back",
-    )(sc, normed_grad, normed_grad_other, middle, attended, seed, mod, mixed, out_weight,
-      normed, qkv, conv, prob, qkv_weight, qkv_weight, qkv_weight, attn_kernel, attn_kernel, attn_kernel)
-
-
-def input_kernel(sc, grad, grad_other, middle_grad, base, mod, near_out, far_out, sums_out):
+    )(sc, att_grad, out_weight, normed, qkv, conv, prob, attn_kernel, attn_kernel, attn_kernel, *deps)
+
+
+def first_back_kernel(count, sc, g0, g1, g2, *rest):
+    weights = rest[0:9]
+    keep, send, grads, weight = rest[9 + count :]
+    core = sc[6]
+    for k, grad in enumerate((g0, g1, g2)):
+        grads[:, 384 * k : 384 * k + 384] = grad[...]
+        for s in range(3):
+            at = 384 * k + LANES * s
+            weight[:, at : at + LANES] = weights[3 * k + s][...]
+    for r in range(0, 1024, 256):
+        split_halves(core, r // 256, dot(grads[r : r + 256, :], weight[...], 1, 1), keep, send)
+
+
+def first_back(sc, grads, qkv_weight, deps=()):
+    def weight_spec(heads, k):
+        return pl.BlockSpec((768, LANES), lambda i, s: (0, 6 * k + 3 * s[6] + heads))
+
+    return pl.pallas_call(
+        functools.partial(first_back_kernel, len(deps)),
+        grid_spec=pltpu.PrefetchScalarGridSpec(
+            num_scalar_prefetch=1,
+            grid=(1,),
+            in_specs=[full(1024, 384)] * 3
+            + [weight_spec(heads, k) for heads in range(3) for k in range(3)]
+            + [ANYWHERE] * len(deps),
+            out_specs=[full(8, 64, 768)] * 2,
+            scratch_shapes=[pltpu.VMEM((1024, 1152), BF), pltpu.VMEM((768, 1152), BF)],
+        ),
+        out_shape=[jax.ShapeDtypeStruct((8, 64, 768), F32), jax.ShapeDtypeStruct((8, 64, 768), BF)],
+        compiler_params=pltpu.CompilerParams(vmem_limit_bytes=VMEM_LIMIT),
+        cost_estimate=pl.CostEstimate(flops=2_000_000_000, bytes_accessed=10_000_000, transcendentals=0),
+        name="first_back",
+    )(sc, *grads, *([qkv_weight] * 9), *deps)
+
+
+def input_kernel(count, sc, grad, grad_other, middle_grad, base, mod, *rest):
+    near_out, far_out, sums_out = rest[count:]
     height, breadth, core = sc[0], sc[1], sc[6]
     scale = 1.0 + mod[1:2, :]
     matrix = to_phase_matrix()
@@ -626,7 +685,7 @@
         for g in range(GROUPS):
             at = 2 * g + local
             token = phase_rows(64, g * 256 + (2 * local + core) * 64)
-            total = grad[at, 0] + grad_other[at].astype(F32)
+            total = grad[at] + grad_other[at].astype(F32)
             unit, inverse = normal(base[at, 0].astype(F32))
             both = total * unit
             d_shift = d_shift + col_sum(total)
@@ -650,15 +709,15 @@
     sums_out[1:2, :] = d_scale
 
 
-def input_grad(sc, grad, grad_other, middle_grad, base, mod):
-    full = lambda *shape: pl.BlockSpec(shape, lambda i, s: (0,) * len(shape))
+def input_grad(sc, grad, grad_other, middle_grad, base, mod, deps=()):
     halves = lambda v: v.reshape(8, 2, 64, 768)
     return pl.pallas_call(
-        input_kernel,
+        functools.partial(input_kernel, len(deps)),
         grid_spec=pltpu.PrefetchScalarGridSpec(
             num_scalar_prefetch=1,
             grid=(1,),
-            in_specs=[half_spec(), full(8, 64, 768), half_spec(), half_spec(), full(8, 768)],
+            in_specs=[full(8, 64, 768), full(8, 64, 768), half_spec(), half_spec(), full(8, 768)]
+            + [ANYWHERE] * len(deps),
             out_specs=[full(256, 768), full(256, 768), full(2, 768)],
         ),
         out_shape=[
@@ -669,7 +728,7 @@
         compiler_params=pltpu.CompilerParams(vmem_limit_bytes=VMEM_LIMIT),
         cost_estimate=pl.CostEstimate(flops=300_000_000, bytes_accessed=6_000_000, transcendentals=0),
         name="input_grad",
-    )(sc, halves(grad), grad_other, halves(middle_grad), halves(base), mod)
+    )(sc, grad, grad_other, halves(middle_grad), halves(base), mod, *deps)
 
 
 def swap(values, axis, bit):
@@ -681,33 +740,198 @@
     return [1 << k for k in range(count.bit_length() - 1)]
 
 
-def halving_order():
-    wide = [("wide", bit) for bit in bits_of(lax.axis_size("wide"))]
-    return wide
-
-
-def has_bit(axis, bit):
-    return (lax.axis_index(axis) & bit) != 0
-
-
-def scatter_sum(block, order):
-    for axis, bit in order:
-        high = has_bit(axis, bit)
-        half = block.shape[0] // 2
-        lower, upper = block[:half], block[half:]
-        send = jnp.where(high, lower, upper)
-        keep = jnp.where(high, upper, lower)
-        got = swap(send, axis, bit)
-        block = (keep.astype(F32) + got.astype(F32)).astype(BF)
-    return block
-
-
-def gather(block, order):
-    for axis, bit in reversed(order):
-        got = swap(block, axis, bit)
-        high = has_bit(axis, bit)
-        block = jnp.concatenate([jnp.where(high, got, block), jnp.where(high, block, got)], axis=0)
-    return block
+def halve_kernel(parts, count, sc, *rest):
+    inputs, (keep1, send1, keep2, send2) = rest[: 4 * parts], rest[4 * parts + count :]
+    half = keep1.shape[0]
+    for part in range(parts):
+        k1, r1, k2, r2 = inputs[4 * part : 4 * part + 4]
+        width = k1.shape[1]
+        cols = slice(part * width, (part + 1) * width)
+        for kept, got, keep, send, bit in ((k1, r1, keep1, send1, sc[8]), (k2, r2, keep2, send2, sc[7])):
+            for place, out in ((bit, keep), (1 - bit, send)):
+                rows = pl.ds(pl.multiple_of(place * half, 16), half)
+                out[:, cols] = (kept[rows, :].astype(F32) + got[rows, :].astype(F32)).astype(BF)
+
+
+def quarter_kernel(count, sc, k1, r1, k2, r2, *rest):
+    outs = rest[count:]
+    width = k1.shape[1]
+    for d, out in enumerate(outs):
+        rows = pl.ds(pl.multiple_of((sc[9] ^ d) * 48, 16), 48)
+        out[:, 0:width] = (k1[rows, :].astype(F32) + r1[rows, :].astype(F32)).astype(BF)
+        out[:, width : 2 * width] = (k2[rows, :].astype(F32) + r2[rows, :].astype(F32)).astype(BF)
+
+
+def total_kernel(count, sc, a, b, c, d, *rest):
+    rest[count][...] = (
+        (a[...].astype(F32) + b[...].astype(F32)) + (c[...].astype(F32) + d[...].astype(F32))
+    ).astype(BF)
+
+
+def glue(kernel, name, sc, operands, shapes, deps):
+    return pl.pallas_call(
+        functools.partial(kernel, len(deps)),
+        grid_spec=pltpu.PrefetchScalarGridSpec(
+            num_scalar_prefetch=1,
+            grid=(1,),
+            in_specs=[full(*v.shape) for v in operands] + [ANYWHERE] * len(deps),
+            out_specs=[full(*shape) for shape in shapes],
+        ),
+        out_shape=[jax.ShapeDtypeStruct(shape, BF) for shape in shapes],
+        cost_estimate=pl.CostEstimate(flops=1_000_000, bytes_accessed=4_000_000, transcendentals=0),
+        compiler_params=pltpu.CompilerParams(vmem_limit_bytes=VMEM_LIMIT),
+        name=name,
+    )(sc, *operands, *deps)
+
+
+def begin(keep1, send1, keep2, send2):
+    for bit in bits_of(lax.axis_size("wide"))[3:]:
+        keep1, send1, keep2, send2 = [
+            (v.astype(F32) + swap(v, "wide", bit).astype(F32)).astype(BF)
+            for v in (keep1, send1, keep2, send2)
+        ]
+    return keep1, swap(send1, "narrow", 2), keep2, swap(send2, "wide", 1)
+
+
+class Flow:
+    def __init__(self, sc, *parts):
+        self.sc = sc
+        self.parts = parts
+        self.width = len(parts) * parts[0][0].shape[1]
+
+    def halve(self, deps=()):
+        operands = [v for part in self.parts for v in part]
+        k1, s1, k2, s2 = glue(
+            functools.partial(halve_kernel, len(self.parts)), "halve", self.sc, operands,
+            [(192, self.width)] * 4, deps,
+        )
+        self.kept = k1, k2
+        self.got = swap(s1, "wide", 1), swap(s2, "narrow", 2)
+        return s1, s2
+
+    def quarter(self, deps=()):
+        outs = glue(
+            quarter_kernel, "quarter", self.sc, (self.kept[0], self.got[0], self.kept[1], self.got[1]),
+            [(48, 2 * self.width)] * 4, deps,
+        )
+        self.kept = outs[0]
+        self.got = [swap(outs[d], "wide", 2 * d) for d in (1, 2, 3)]
+        return tuple(outs[1:])
+
+    def total(self, deps=()):
+        (self.own,) = glue(
+            total_kernel, "total", self.sc, (self.kept, *self.got), [(48, 2 * self.width)], deps
+        )
+        return (self.own,)
+
+    def gather_one(self):
+        every = [self.own, *(swap(self.own, "wide", 2 * d) for d in (1, 2, 3))]
+        self.kept = tuple(
+            jnp.concatenate([v[:, at : at + self.width] for v in every], axis=0) for at in (0, self.width)
+        )
+        self.got = swap(self.kept[0], "wide", 1), swap(self.kept[1], "narrow", 2)
+
+    def gather_two(self):
+        self.kept = tuple(jnp.concatenate(pair, axis=0) for pair in zip(self.kept, self.got))
+        self.got = swap(self.kept[0], "narrow", 2), swap(self.kept[1], "wide", 1)
+
+    def gather_three(self):
+        self.kept = jnp.concatenate(
+            [jnp.concatenate(pair, axis=0) for pair in zip(self.kept, self.got)], axis=1
+        )
+        self.got = swap(self.kept, "narrow", 1)
+
+    def gather_all(self):
+        return lax.all_gather(self.own, ("wide", "narrow"), axis=0, tiled=False)
+
+
+def feed_done_kernel(sc, *refs):
+    up_out, down_out = refs[4:]
+    for core in range(2):
+        one, two = refs[2 * core : 2 * core + 2]
+        up_out[:, 1536 * core : 1536 * core + 1536] = one[0].astype(F32)
+        for half in range(2):
+            down_out[2 * core + half] = two[0, :, 768 * half : 768 * half + 768].astype(F32)
+
+
+def feed_done(sc, gathered):
+    def device(x, y, z, core):
+        return (2 * z + y) * 4 + 2 * x + core
+
+    def one(core):
+        return pl.BlockSpec(
+            (1, 48, 1536), lambda i, s: (device(i // 8, (i // 4) % 2, i % 4, core), 0, 0)
+        )
+
+    def two(core):
+        return pl.BlockSpec(
+            (1, 48, 1536), lambda i, s: (device((i // 4) % 2, i // 8, i % 4, core), 0, 1)
+        )
+
+    up, down = pl.pallas_call(
+        feed_done_kernel,
+        grid_spec=pltpu.PrefetchScalarGridSpec(
+            num_scalar_prefetch=1,
+            grid=(16,),
+            in_specs=[one(0), two(0), one(1), two(1)],
+            out_specs=[
+                pl.BlockSpec((48, 3072), lambda i, s: (i, 0)),
+                pl.BlockSpec((4, 48, 768), lambda i, s: (0, i, 0)),
+            ],
+        ),
+        out_shape=[
+            jax.ShapeDtypeStruct((768, 3072), F32),
+            jax.ShapeDtypeStruct((4, 768, 768), F32),
+        ],
+        compiler_params=pltpu.CompilerParams(vmem_limit_bytes=VMEM_LIMIT),
+        cost_estimate=pl.CostEstimate(flops=1_000_000, bytes_accessed=28_000_000, transcendentals=0),
+        name="feed_done",
+    )(sc, *([gathered] * 4))
+    return up, down.reshape(3072, 768)
+
+
+def attend_done_kernel(sc, one, two, other_one, other_two, qkv_grad, out_grad):
+    def write(core, first, second):
+        for at, part in enumerate((first[:, 0:384], first[:, 384:768], second[:, 384:768])):
+            for k in range(3):
+                dest = 768 * k + 384 * core + LANES * at
+                qkv_grad[:, dest : dest + LANES] = part[:, LANES * k : LANES * k + LANES].astype(F32)
+        out_grad[core] = second[:, 0:384].astype(F32)
+
+    @pl.when(sc[6] == 0)
+    def _():
+        write(0, one[...], two[...])
+        write(1, other_one[...], other_two[...])
+
+    @pl.when(sc[6] != 0)
+    def _():
+        write(0, other_one[...], other_two[...])
+        write(1, one[...], two[...])
+
+
+def attend_done(sc, own, other):
+    one = pl.BlockSpec((48, 768), lambda i, s: (i ^ s[10], 0))
+    two = pl.BlockSpec((48, 768), lambda i, s: (i ^ s[11], 1))
+    qkv_grad, out_grad = pl.pallas_call(
+        attend_done_kernel,
+        grid_spec=pltpu.PrefetchScalarGridSpec(
+            num_scalar_prefetch=1,
+            grid=(16,),
+            in_specs=[one, two] * 2,
+            out_specs=[
+                pl.BlockSpec((48, 2304), lambda i, s: (i, 0)),
+                pl.BlockSpec((2, 48, 384), lambda i, s: (0, i % 8, i // 8)),
+            ],
+        ),
+        out_shape=[
+            jax.ShapeDtypeStruct((768, 2304), F32),
+            jax.ShapeDtypeStruct((2, 384, 768), F32),
+        ],
+        compiler_params=pltpu.CompilerParams(vmem_limit_bytes=VMEM_LIMIT),
+        cost_estimate=pl.CostEstimate(flops=1_000_000, bytes_accessed=14_000_000, transcendentals=0),
+        name="attend_done",
+    )(sc, own, own, other, other)
+    return qkv_grad, out_grad.reshape(768, 768)
 
 
 def sum_all(values, order):
@@ -742,9 +966,11 @@
     modul = jnp.where(stays, conditioning, from_right).astype(F32).reshape(6, 768)
     factor = 1024.0 / (sides[0] * sides[1]).astype(F32)
     mod = jnp.concatenate([modul, jnp.full((2, 768), factor, F32)], axis=0)
+    at_y, at_z = wide_at % 2, (wide_at // 2) % 4
     sc = jnp.stack(
         [sides[0], sides[1], 2 * pair + core, 2 * (1 - pair) + core, 2 * pair + 1 - core,
-         2 * (1 - pair) + 1 - core, core, pair]
+         2 * (1 - pair) + 1 - core, core, pair, at_y, at_z,
+         8 * pair + 4 * at_y + at_z, 8 * at_y + 4 * pair + at_z]
     ).astype(jnp.int32)
     attn_k = attn_kernel.reshape(9, -1)
     ffn_k = ffn_kernel.reshape(9, -1)
@@ -754,20 +980,42 @@
     attended, middle, normed_two, d_branch, seed = project_out(
         sc, mixed, mixed_other, base, out_weight, mod, seed_pieces
     )
-    down_a, up_a, ffn_a, branch, d_normed = feed(
+    *streams, ffn_a, branch, d_normed = feed(
         sc, normed_two, d_branch, up_weight, down_weight, ffn_k, 0, None
     )
-    down_b, up_b, ffn_b, branch, d_normed = feed(
+    part_a = begin(*streams)
+    *streams, ffn_b, branch, branch_send, d_normed, d_normed_send = feed(
         sc, normed_two, d_branch, up_weight, down_weight, ffn_k, 1, (branch, d_normed)
     )
-
-    def other_half(values):
-        cut = values.reshape(8, 2, 64, 768)
-        return lax.dynamic_index_in_dim(cut, 1 - core, 1, keepdims=False).astype(BF)
-
-    d_normed_other = swap(d_normed.astype(BF), "narrow", 1)
-    branch_other = swap(other_half(branch), "narrow", 1)
-    near, far, d_gate_two = finish(sc, middle, branch, branch_other, seed, mod)
+    d_normed_other = swap(d_normed_send, "narrow", 1)
+    part_b = begin(*streams)
+    branch_other = swap(branch_send, "narrow", 1)
+    d_middle, d_att, sums_two, *out_parts = norm_back(
+        sc, d_normed, d_normed_other, middle, attended, seed, mod, mixed
+    )
+
+    def back(heads, axis, deps):
+        return attend_back(
+            sc, heads, axis, d_att, out_weight, normed_one, qkv, conv, prob, attn_k, deps
+        )
+
+    feeds = Flow(sc, part_a, part_b)
+    made = feeds.halve((d_att,))
+    g0, kg0, *parts = back(0, 7, made)
+    part_c = begin(*parts, *out_parts)
+    made = feeds.quarter((g0,))
+    g1, kg1, *parts_one = back(1, 7, made)
+    g2, kg2, *parts_two = back(2, 8, (g1,))
+    part_d = begin(*parts_one, *parts_two)
+    made = feeds.total((g2,))
+    gathered = feeds.gather_all()
+    d_first, d_first_send = first_back(sc, (g0, g1, g2), qkv_weight, made)
+    d_first_other = swap(d_first_send, "narrow", 1)
+    attends = Flow(sc, part_c, part_d)
+    made = attends.halve((d_first,))
+
+    near, far, d_gate_two = finish(sc, middle, branch, branch_other, seed, mod, made)
+    made = attends.quarter((near,))
     far = swap(far, "narrow", 2)
 
     def as_output(near, far):
@@ -776,12 +1024,8 @@
         return jnp.stack([first, second]).reshape(tokens.shape)
 
     block_out = as_output(near, far)
-    d_middle, sums_two, attn_bundle, attn_kg, d_first = attend_back(
-        sc, d_normed, d_normed_other, middle, attended, seed, mod, mixed, out_weight,
-        normed_one, qkv, conv, prob, qkv_weight, attn_k
-    )
-    d_first_other = swap(other_half(d_first), "narrow", 1)
-    near, far, sums_one = input_grad(sc, d_first, d_first_other, d_middle, base, mod)
+    near, far, sums_one = input_grad(sc, d_first, d_first_other, d_middle, base, mod, made)
+    attends.total((near,))
     tokens_grad = as_output(near, swap(far, "narrow", 2))
 
     cond = jnp.concatenate(
@@ -794,41 +1038,18 @@
     cond = sum_all(cond, [("narrow", 1), ("narrow", 2)])
 
     chips = [("wide", bit) for bit in bits_of(wide_count)] + [("narrow", 2)]
-    order = [("narrow", 2)] + [("wide", bit) for bit in bits_of(wide_count)]
-
-    def reduce(block):
-        half = gather(scatter_sum(block, order), order)
-        other = swap(half, "narrow", 1)
-        return jnp.where(core == 0, half, other), jnp.where(core == 0, other, half)
-
-    down_a0, down_a1 = reduce(down_a)
-    up_a0, up_a1 = reduce(up_a)
-    down_b0, down_b1 = reduce(down_b)
-    up_b0, up_b1 = reduce(up_b)
-    attn0, attn1 = reduce(attn_bundle)
-    down_grad = jnp.concatenate([down_a0, down_b0, down_a1, down_b1], axis=0).astype(F32)
-    up_grad = jnp.concatenate([up_a0, up_b0, up_a1, up_b1], axis=1).astype(F32)
-    qkv_grad = jnp.concatenate(
-        [v[:, 384 * s : 384 * s + 384] for s in range(3) for v in (attn0, attn1)], axis=1
-    ).astype(F32)
-    out_grad = jnp.concatenate(
-        [
-            jnp.concatenate([v[0:384, 1152:], v[384:768, 1152:]], axis=1)
-            for v in (attn0, attn1)
-        ],
-        axis=0,
-    ).astype(F32)
-
-    def kernel_grads(values):
-        half = sum_all(values, chips)
-        other = swap(half, "narrow", 1)
-        return jnp.where(core == 0, half, other), jnp.where(core == 0, other, half)
-
-    ffn0, ffn1 = kernel_grads(jnp.concatenate([ffn_a, ffn_b], axis=1))
-    ffn_grad = jnp.concatenate([ffn0, ffn1], axis=1).reshape(ffn_kernel.shape)
-    attn_kg = attn_kg.reshape(3, 9, 3, 128).transpose(1, 2, 0, 3).reshape(9, 3, 384)
-    kg0, kg1 = kernel_grads(attn_kg)
-    attn_grad = jnp.concatenate([kg0, kg1], axis=2).reshape(attn_kernel.shape)
+    small = sum_all(jnp.concatenate([ffn_a, ffn_b, kg0, kg1, kg2], axis=1), chips)
+    small_other = swap(small, "narrow", 1)
+    first, second = jnp.where(core == 0, small, small_other), jnp.where(core == 0, small_other, small)
+    ffn_grad = jnp.concatenate([first[:, :1536], second[:, :1536]], axis=1).reshape(ffn_kernel.shape)
+    attn_grad = jnp.stack([first[:, 1536:], second[:, 1536:]], axis=1).reshape(9, 2, 3, 3, LANES)
+    attn_grad = attn_grad.transpose(0, 3, 1, 2, 4).reshape(attn_kernel.shape)
+
+    attends.gather_one()
+    attends.gather_two()
+    attends.gather_three()
+    qkv_grad, out_grad = attend_done(sc, attends.kept, attends.got)
+    up_grad, down_grad = feed_done(sc, gathered)
 
     return (
         block_out, tokens_grad, cond[0:5].reshape(1, -1), cond[5:6],

time: 474 us -> 411 us (0.87)
  waiting for transfers between devices: 174 us -> 101 us
  Pallas kernels: 147 us -> 206 us
  other arithmetic: 62.1 us -> 4.85 us
  between operations: 4.09 us -> 16.9 us
  starting transfers between devices: 55 us -> 47.5 us
  local copies, waits for them, and re-layouts: 21.6 us -> 26.8 us
    ppermute x69 -> x45, waiting for transfers between devices: 174 us -> 100 us  [swap(): return lax.ppermute(values, axis, [(i, i ^ bit) for i in range(count)])]
    pallas_call x5 -> x17, Pallas kernels: 110 us -> 169 us  [the longest x2 55.2 us: feed(): pl.pallas_call(functools.partial(feed_kernel, len(deps), first), grid_spe...]
    convert_element_type x25 -> x0, other arithmetic: 25.5 us -> none  [the longest x20 8.83 us: scatter_sum(): block = (keep.astype(F32) + got.astype(F32)).astype(BF)]
    select_n x47 -> x1, other arithmetic: 24.8 us -> 0.03 us  [on_device(): jnp.where(core == 0, small, small_other)]
    unnamed x90 -> x106, local copies, waits for them, and re-layouts: 5.9 us -> 14.9 us
    concatenate x22 -> x4, other arithmetic: 9.27 us -> 1.49 us  [the longest x1 1.44 us: gather_three(): jnp.concatenate([jnp.concatenate(pair, axis=0) for pair in zip(self.kept,...]
    ppermute x69 -> x45, starting transfers between devices: 50 us -> 43.7 us  [swap(): return lax.ppermute(values, axis, [(i, i ^ bit) for i in range(count)])]
    convert_element_type x2 -> x0, local copies, waits for them, and re-layouts: 4.91 us -> none  [other_half(): return lax.dynamic_index_in_dim(cut, 1 - core, 1, keepdims=False).astype(BF)]
  transfers between devices with their start and end apart: 71 -> 48, of which waited for: 35 -> 20; matrix products, arithmetic and copies ran while one was open for 15% -> 5% of each run, Pallas kernels for 18% -> 28%
where the time goes in v2:
time: 411 us; the launch traced here: 403 us
  Pallas kernels  206 us (50%)
  waiting for transfers between devices  101 us (25%)
  starting transfers between devices  47.5 us (12%)
  local copies, waits for them, and re-layouts  26.8 us (7%)
  between operations  16.9 us (4%)
  other arithmetic  4.85 us (1%)
    ppermute x45, waiting for transfers between devices, swap(): return lax.ppermute(values, axis, [(i, i ^ bit) for i in range(count)])  100 us
    pallas_call x2, Pallas kernels, feed(): pl.pallas_call(functools.partial(feed_kernel, len(deps), first), grid_spe...  55.2 us
    ppermute x45, starting transfers between devices, swap(): return lax.ppermute(values, axis, [(i, i ^ bit) for i in range(count)])  43.7 us
    pallas_call x3, Pallas kernels, attend_back(): pl.pallas_call(functools.partial(attend_back_kernel, len(deps), axis), gr...  35.1 us
    pallas_call x1, Pallas kernels, attend(): pl.pallas_call(attend_kernel, grid_spec=pltpu.PrefetchScalarGridSpec(num_...  24.7 us
    pallas_call x6, Pallas kernels, glue(): pl.pallas_call(functools.partial(kernel, len(deps)), grid_spec=pltpu.Pref...  20.4 us
    pallas_call x1, Pallas kernels, feed_done(): pl.pallas_call(feed_done_kernel, grid_spec=pltpu.PrefetchScalarGridSpec(n...  15.3 us
    unnamed x106, local copies, waits for them, and re-layouts  14.9 us
  transfers between devices with their start and end apart: 48, of which 20 were waited for; matrix products, arithmetic and copies ran while one was open for 5% of the time, Pallas kernels for 28%

profile of v2, /device:TPU:0, one launch (start us, length us, event | category | flops | bytes accessed | tf_op | source)
XLA Modules:
  0.0 403.5 jit_solution(15498597075934819805)
XLA Ops:
  8.6 3.0 collective-permute-start
  12.9 7.7 %collective-permute-done.p1 = bf16[256,768]{1,0:T(8,128)(2,1)S(1)} collective-permute-done((bf16[256,768]{1,0:T(8,128)(2,1)S(1)}, bf16[256,768]{1,0:T(8,128)(2,1)S(1)}, u32[]{:S(2)}, u32[]{:S(2)}) %collective-permute-start) | collective-permute-done | bytes 393248 | tf_op jit(solution)/shard_map/ppermute | solution.py:736
  30.6 24.7 %attend.1 = (bf16[1024,768]{1,0:T(8,128)(2,1)}, bf16[1024,768]{1,0:T(8,128)(2,1)}, bf16[3,1024,384]{2,1,0:T(8,128)(2,1)}, bf16[3,1024,384]{2,1,0:T(8,128)(2,1)},...) custom-call(s32[12]{0:T(128)} %stack.70.sc, bf16[256,768]{1,0:T(8,128)(2,1)} %copy-done.3, ...), custom_call_target="tpu_custom_call" | custom-call | flops 3000000000 | bytes 20000000 | tf_op jit(solution)/shard_map/attend/pallas_call | solution.py:215
  60.1 12.6 %project_out.1 = (bf16[1024,768]{1,0:T(8,128)(2,1)}, f32[1024,768]{1,0:T(8,128)}, bf16[1024,768]{1,0:T(8,128)(2,1)}, bf16[1024,768]{1,0:T(8,128)(2,1)}, bf16[1024,768]{1,0:T(8,128)(2,1)}) custom-call(s32[12]{0:T(128)} %stack.70.sc, bf16[1024,384]{1,0:T(8,128)(2,1)} %get-tuple-element.82.mixed_own.mixed, bf16[1024,384]{1,0:T(8,128)(2,1)} %copy-done.43, ...), custom_call_target="tpu_custom_call" | custom-call | flops 2000000000 | bytes 20000000 | tf_op jit(solution)/shard_map/project_out/pallas_call | solution.py:285
  72.6 26.7 %feed.2 = (bf16[384,768]{1,0:T(8,128)(2,1)}, bf16[384,768]{1,0:T(8,128)(2,1)}, bf16[384,768]{1,0:T(8,128)(2,1)}, bf16[384,768]{1,0:T(8,128)(2,1)}, f32[9,768]{1,...) custom-call(s32[12]{0:T(128)} %stack.70.sc, bf16[1024,768]{1,0:T(8,128)(2,1)} %get-tuple-element.85.normed, ...), custom_call_target="tpu_custom_call" | custom-call | flops 15000000512 | bytes 60000000 | tf_op jit(solution)/shard_map/feed/pallas_call | solution.py:398
  99.4 28.5 %feed.3 = (bf16[384,768]{1,0:T(8,128)(2,1)}, bf16[384,768]{1,0:T(8,128)(2,1)}, bf16[384,768]{1,0:T(8,128)(2,1)}, bf16[384,768]{1,0:T(8,128)(2,1)}, f32[9,768]{1,...) custom-call(s32[12]{0:T(128)} %stack.70.sc, ...), custom_call_target="tpu_custom_call" | custom-call | flops 15000000512 | bytes 60000000 | tf_op jit(solution)/shard_map/feed/pallas_call | solution.py:398
  133.3 12.6 %norm_back.1 = (f32[1024,768]{1,0:T(8,128)}, bf16[1024,768]{1,0:T(8,128)(2,1)}, f32[3,768]{1,0:T(4,128)}, bf16[384,384]{1,0:T(8,128)(2,1)}, bf16[384,384]{1,0:T(8,128)(2,1)}) custom-call(s32[12]{0:T(128)} %stack.70.sc, f32[1024,768]{1,0:T(8,128)} %get-tuple-element.92.normed_grad, bf16[1024,768]{1,0:T(8,128)(2,1)} %copy-done.41, ...), custom_call_target="tpu_custom_call" | custom-call | flops 4000000000 | bytes 30000000 | tf_op jit(solution)/shard_map/norm_back/pallas_call | solution.py:530
  146.0 10.5 %collective-permute-done.10.rest_1_ = bf16[384,768]{1,0:T(8,128)(2,1)S(1)} collective-permute-done((bf16[384,768]{1,0:T(8,128)(2,1)}, bf16[384,768]{1,0:T(8,128)(2,1)S(1)}, u32[]{:S(2)}, u32[]{:S(2)}) %collective-permute-start.10) | collective-permute-done | bytes 589856 | tf_op jit(solution)/shard_map/ppermute | solution.py:736
  157.5 5.0 %halve.2 = (bf16[192,1536]{1,0:T(8,128)(2,1)}, bf16[192,1536]{1,0:T(8,128)(2,1)}, bf16[192,1536]{1,0:T(8,128)(2,1)}, bf16[192,1536]{1,0:T(8,128)(2,1)}) custom-call(s32[12]{0:T(128)} %stack.70.sc, bf16[384,768]{1,0:T(8,128)(2,1)} %get-tuple-element.100.rest_0_, bf16[384,768]{1,0:T(8,128)(2,1)} %copy-done.11, bf16[384,768]{1,0:T(8,128)(2,1)} %get-tuple-element.102.rest_2_, ...), custom_call_target="tpu_custom_call" | custom-call | flops 1000000 | bytes 4000000 | tf_op jit(solution)/shard_map/halve/pallas_call | solution.py:772
  165.6 11.8 %attend_back.3 = (bf16[1024,384]{1,0:T(8,128)(2,1)}, f32[9,384]{1,0:T(8,128)}, bf16[384,384]{1,0:T(8,128)(2,1)}, bf16[384,384]{1,0:T(8,128)(2,1)}) custom-call(s32[12]{0:T(128)} %stack.70.sc, bf16[1024,768]{1,0:T(8,128)(2,1)} %get-tuple-element.95.rest_8_.att_grad, bf16[768,768]{1,0:T(8,128)(2,1)} %out_weight.7, bf16[1024,768]{1,0:T(8,128)(2,1)} %get-tuple-element.96.normed, ...), custom_call_target="tpu_custom_call" | custom-call | flops 6000000000 | bytes 30000000 | tf_op jit(solution)/shard_map/attend_back/pallas_call | solution.py:611
  179.5 3.4 quarter.2
  187.3 11.6 %attend_back.4 = (bf16[1024,384]{1,0:T(8,128)(2,1)}, f32[9,384]{1,0:T(8,128)}, bf16[384,384]{1,0:T(8,128)(2,1)}, bf16[384,384]{1,0:T(8,128)(2,1)}) custom-call(s32[12]{0:T(128)} %stack.70.sc, bf16[1024,768]{1,0:T(8,128)(2,1)} %get-tuple-element.95.rest_8_.att_grad, bf16[768,768]{1,0:T(8,128)(2,1)} %out_weight.7, bf16[1024,768]{1,0:T(8,128)(2,1)} %get-tuple-element.96.normed, ...), custom_call_target="tpu_custom_call" | custom-call | flops 6000000000 | bytes 30000000 | tf_op jit(solution)/shard_map/attend_back/pallas_call | solution.py:611
  198.9 11.7 %attend_back.5 = (bf16[1024,384]{1,0:T(8,128)(2,1)}, f32[9,384]{1,0:T(8,128)}, bf16[384,384]{1,0:T(8,128)(2,1)}, bf16[384,384]{1,0:T(8,128)(2,1)}) custom-call(s32[12]{0:T(128)} %stack.70.sc, bf16[1024,768]{1,0:T(8,128)(2,1)} %get-tuple-element.95.rest_8_.att_grad, bf16[768,768]{1,0:T(8,128)(2,1)} %out_weight.7, bf16[1024,768]{1,0:T(8,128)(2,1)} %get-tuple-element.96.normed, ...), custom_call_target="tpu_custom_call" | custom-call | flops 6000000000 | bytes 30000000 | tf_op jit(solution)/shard_map/attend_back/pallas_call | solution.py:611
  211.5 2.9 total.2.rest_9_
  218.6 6.5 %first_back.1 = (f32[8,64,768]{2,1,0:T(8,128)}, bf16[8,64,768]{2,1,0:T(8,128)(2,1)}) custom-call(s32[12]{0:T(128)} %stack.70.sc, bf16[1024,384]{1,0:T(8,128)(2,1)} %get-tuple-element.116.rest_0_.g0, bf16[1024,384]{1,0:T(8,128)(2,1)} %get-tuple-element.122.rest_0_.g1, bf16[1024,384]{1,0:T(8,128)(2,1)} %get-tuple-element.125.rest_0_.g2, ...), custom_call_target="tpu_custom_call" | custom-call | flops 2000000000 | bytes 10000000 | tf_op jit(solution)/shard_map/first_back/pallas_call | solution.py:658
  225.2 7.9 %collective-permute-done.18.rest_5_ = bf16[384,384]{1,0:T(8,128)(2,1)S(1)} collective-permute-done((bf16[384,384]{1,0:T(8,128)(2,1)}, bf16[384,384]{1,0:T(8,128)(2,1)S(1)}, u32[]{:S(2)}, u32[]{:S(2)}) %collective-permute-start.18) | collective-permute-done | bytes 294944 | tf_op jit(solution)/shard_map/ppermute | solution.py:736
  233.9 3.5 halve.3
  241.1 5.5 %finish.1 = (bf16[256,768]{1,0:T(8,128)(2,1)}, bf16[256,768]{1,0:T(8,128)(2,1)}, f32[1,768]{1,0:T(1,128)}) custom-call(s32[12]{0:T(128)} %stack.70.sc, f32[8,2,64,768]{3,2,1,0:T(8,128)} %bitcast.45, f32[8,64,768]{2,1,0:T(8,128)} %get-tuple-element.89.branch, bf16[8,64,768]{2,1,0:T(8,128)(2,1)} %copy-done.7, bf16[8,2,64,768]{3,2,1,0:T(8,128)(2,1)} %bitcast.52, ...), custom_call_target="tpu_custom_call" | custom-call | flops 300000000 | bytes 6000000 | tf_op jit(solution)/shard_map/finish/pallas_call | solution.py:475
  255.9 3.4 collective-permute-start.32
  260.3 6.0 %input_grad.1 = (bf16[256,768]{1,0:T(8,128)(2,1)}, bf16[256,768]{1,0:T(8,128)(2,1)}, f32[2,768]{1,0:T(2,128)}) custom-call(s32[12]{0:T(128)} %stack.70.sc, f32[8,64,768]{2,1,0:T(8,128)} %get-tuple-element.127.rest_8_.grad, bf16[8,64,768]{2,1,0:T(8,128)(2,1)} %copy-done.6, f32[8,2,64,768]{3,2,1,0:T(8,128)} %bitcast.46, bf16[8,2,64,768]{3,2,1,0:T(8,128)(2,1)} %bitcast.51, ...), custom_call_target="tpu_custom_call" | custom-call | flops 300000000 | bytes 6000000 | tf_op jit(solution)/shard_map/input_grad/pallas_call | solution.py:714
  266.3 6.7 %collective-permute-done.32.c = bf16[48,1536]{1,0:T(8,128)(2,1)S(1)} collective-permute-done((bf16[48,1536]{1,0:T(8,128)(2,1)}, bf16[48,1536]{1,0:T(8,128)(2,1)S(1)}, u32[]{:S(2)}, u32[]{:S(2)}) %collective-permute-start.32) | collective-permute-done | bytes 147488 | tf_op jit(solution)/shard_map/ppermute | solution.py:736
  273.7 2.8 total.3
  282.5 13.6 %collective-permute-done.34 = bf16[48,1536]{1,0:T(8,128)(2,1)S(1)} collective-permute-done((bf16[48,1536]{1,0:T(8,128)(2,1)}, bf16[48,1536]{1,0:T(8,128)(2,1)S(1)}, u32[]{:S(2)}, u32[]{:S(2)}) %collective-permute-start.34) | collective-permute-done | bytes 147488 | tf_op jit(solution)/shard_map/ppermute | solution.py:736
  296.8 10.7 %collective-permute-done.35 = bf16[48,1536]{1,0:T(8,128)(2,1)S(1)} collective-permute-done((bf16[48,1536]{1,0:T(8,128)(2,1)}, bf16[48,1536]{1,0:T(8,128)(2,1)S(1)}, u32[]{:S(2)}, u32[]{:S(2)}) %collective-permute-start.35) | collective-permute-done | bytes 147488 | tf_op jit(solution)/shard_map/ppermute | solution.py:736
  312.6 3.2 collective-permute-done.39
  317.6 2.8 collective-permute-done.37
  324.2 7.2 %collective-permute-done.43 = f32[9,2688]{1,0:T(8,128)S(1)} collective-permute-done((f32[9,2688]{1,0:T(8,128)S(1)}, f32[9,2688]{1,0:T(8,128)S(1)}, u32[]{:S(2)}, u32[]{:S(2)}) %collective-permute-start.43) | collective-permute-done | bytes 96800 | tf_op jit(solution)/shard_map/ppermute | solution.py:736
  331.7 6.9 %collective-permute-done.44 = f32[9,2688]{1,0:T(8,128)S(1)} collective-permute-done((f32[9,2688]{1,0:T(8,128)S(1)}, f32[9,2688]{1,0:T(8,128)S(1)}, u32[]{:S(2)}, u32[]{:S(2)}) %collective-permute-start.44) | collective-permute-done | bytes 96800 | tf_op jit(solution)/shard_map/ppermute | solution.py:736
  340.8 3.3 collective-permute-done.45
  357.0 9.1 %collective-permute-done.30 = f32[6,768]{1,0:T(8,128)S(1)} collective-permute-done((f32[6,768]{1,0:T(8,128)S(1)}, f32[6,768]{1,0:T(8,128)S(1)}, u32[]{:S(2)}, u32[]{:S(2)}) %collective-permute-start.30) | collective-permute-done | bytes 18464 | tf_op jit(solution)/shard_map/ppermute | solution.py:736
  368.7 12.4 %attend_done.1 = (f32[768,2304]{1,0:T(8,128)}, f32[2,384,768]{2,1,0:T(8,128)}) custom-call(s32[12]{0:T(128)} %stack.70.sc, bf16[768,1536]{1,0:T(8,128)(2,1)} %copy-done.2, bf16[768,1536]{1,0:T(8,128)(2,1)} %copy-done.2, bf16[768,1536]{1,0:T(8,128)(2,1)} %collective-permute-done.41.other_one.other_two, ...), custom_call_target="tpu_custom_call" | custom-call | flops 1000000 | bytes 14000000 | tf_op jit(solution)/shard_map/attend_done/pallas_call | solution.py:915
  381.1 15.3 %feed_done.1 = (f32[768,3072]{1,0:T(8,128)}, f32[4,768,768]{2,1,0:T(8,128)}) custom-call(s32[12]{0:T(128)} %stack.70.sc, bf16[32,48,3072]{2,1,0:T(8,128)(2,1)} %bitcast.41, bf16[32,48,3072]{2,1,0:T(8,128)(2,1)} %bitcast.42, bf16[32,48,3072]{2,1,0:T(8,128)(2,1)} %bitcast.43, bf16[32,48,3072]{2,1,0:T(8,128)(2,1)} %bitcast.44), custom_call_target="tpu_custom_call" | custom-call | flops 1000000 | bytes 28000000 | tf_op jit(solution)/shard_map/feed_done/pallas_call | solution.py:871
  (235 shorter events, 86.9 us)
Async XLA Ops:
  7.2 373.8 %all-gather.3.cloned.1.call-start = ((), (), s32[]{:S(2)}) async-start(), calls=%async_computation | async-start | bytes 9732096 | tf_op jit(solution)/shard_map/all_gather | solution.py:845
  8.6 12.1 %collective-permute-start = (bf16[256,768]{1,0:T(8,128)(2,1)S(1)}, bf16[256,768]{1,0:T(8,128)(2,1)S(1)}, u32[]{:S(2)}, u32[]{:S(2)}) collective-permute-start(bf16[256,768]{1,0:T(8,128)(2,1)S(1)} %get-tuple-element.160), channel_id=1, source_target_pairs={{0,2},{1,3},{2,0},{3,1},{4,6},{5,7},{6,4},{7,5},{8,10},{9,11},{10,... | collective-permute-start | bytes 1179656 | tf_op jit(solution)/shard_map/ppermute | solution.py:736
  11.6 16.8 %collective-permute-start.3 = (bf16[1,4608]{1,0:T(2,128)(2,1)S(1)}, bf16[1,4608]{1,0:T(2,128)(2,1)S(1)}, u32[]{:S(2)}, u32[]{:S(2)}) collective-permute-start(bf16[1,4608]{1,0:T(2,128)(2,1)S(1)} %copy-done.38), channel_id=1, source_target_pairs={{4,0},{8,4},{12,8},{16,12},{20,16},{24,20},{28,24},{5,1},{9,5},{13... | collective-permute-start | bytes 27656 | tf_op jit(solution)/shard_map/ppermute | solution.py:965
  12.9 16.2 %collective-permute-start.1 = (bf16[256,768]{1,0:T(8,128)(2,1)S(1)}, bf16[256,768]{1,0:T(8,128)(2,1)S(1)}, u32[]{:S(2)}, u32[]{:S(2)}) collective-permute-start(bf16[256,768]{1,0:T(8,128)(2,1)S(1)} %get-tuple-element.161.p0), channel_id=1, source_target_pairs={{0,1},{1,0},{2,3},{3,2},{4,5},{5,4},{6,7},{7,6},{8,9},{9,8},{10,11... | collective-permute-start | bytes 1179656 | tf_op jit(solution)/shard_map/ppermute | solution.py:736
  20.8 35.2 %collective-permute-start.5 = (bf16[256,768]{1,0:T(8,128)(2,1)S(1)}, bf16[256,768]{1,0:T(8,128)(2,1)}, u32[]{:S(2)}, u32[]{:S(2)}) collective-permute-start(bf16[256,768]{1,0:T(8,128)(2,1)S(1)} %get-tuple-element.158), channel_id=1, source_target_pairs={{0,2},{1,3},{2,0},{3,1},{4,6},{5,7},{6,4},{7,5},{8,10},{9,11},{10,... | collective-permute-start | bytes 1179656 | tf_op jit(solution)/shard_map/ppermute | solution.py:736
  128.1 17.9 %collective-permute-start.12 = (bf16[384,768]{1,0:T(8,128)(2,1)}, bf16[384,768]{1,0:T(8,128)(2,1)S(1)}, u32[]{:S(2)}, u32[]{:S(2)}) collective-permute-start(bf16[384,768]{1,0:T(8,128)(2,1)} %get-tuple-element.105), channel_id=1, source_target_pairs={{0,2},{1,3},{2,0},{3,1},{4,6},{5,7},{6,4},{7,5},{8,10},{9,11},{10,... | collective-permute-start | bytes 1769480 | tf_op jit(solution)/shard_map/ppermute | solution.py:736
  128.4 17.6 %collective-permute-start.13 = (bf16[384,768]{1,0:T(8,128)(2,1)}, bf16[384,768]{1,0:T(8,128)(2,1)S(1)}, u32[]{:S(2)}, u32[]{:S(2)}) collective-permute-start(bf16[384,768]{1,0:T(8,128)(2,1)} %get-tuple-element.107), channel_id=1, source_target_pairs={{0,4},{4,0},{8,12},{12,8},{16,20},{20,16},{24,28},{28,24},{1,5},{5... | collective-permute-start | bytes 1769480 | tf_op jit(solution)/shard_map/ppermute | solution.py:736
  130.2 26.3 %collective-permute-start.10 = (bf16[384,768]{1,0:T(8,128)(2,1)}, bf16[384,768]{1,0:T(8,128)(2,1)S(1)}, u32[]{:S(2)}, u32[]{:S(2)}) collective-permute-start(bf16[384,768]{1,0:T(8,128)(2,1)} %get-tuple-element.101), channel_id=1, source_target_pairs={{0,2},{1,3},{2,0},{3,1},{4,6},{5,7},{6,4},{7,5},{8,10},{9,11},{10,... | collective-permute-start | bytes 1769480 | tf_op jit(solution)/shard_map/ppermute | solution.py:736
  131.7 24.9 %collective-permute-start.11 = (bf16[384,768]{1,0:T(8,128)(2,1)}, bf16[384,768]{1,0:T(8,128)(2,1)S(1)}, u32[]{:S(2)}, u32[]{:S(2)}) collective-permute-start(bf16[384,768]{1,0:T(8,128)(2,1)} %get-tuple-element.103), channel_id=1, source_target_pairs={{0,4},{4,0},{8,12},{12,8},{16,20},{20,16},{24,28},{28,24},{1,5},{5... | collective-permute-start | bytes 1769480 | tf_op jit(solution)/shard_map/ppermute | solution.py:736
  162.5 14.9 %collective-permute-start.16 = (bf16[192,1536]{1,0:T(8,128)(2,1)}, bf16[192,1536]{1,0:T(8,128)(2,1)S(1)}, u32[]{:S(2)}, u32[]{:S(2)}) collective-permute-start(bf16[192,1536]{1,0:T(8,128)(2,1)} %get-tuple-element.108.rest_0_), channel_id=1, source_target_pairs={{0,4},{4,0},{8,12},{12,8},{16,20},{20,16},{24,28},{28,24},{1,5},{5... | collective-permute-start | bytes 1769480 | tf_op jit(solution)/shard_map/ppermute | solution.py:736
  164.1 14.6 %collective-permute-start.17 = (bf16[192,1536]{1,0:T(8,128)(2,1)}, bf16[192,1536]{1,0:T(8,128)(2,1)S(1)}, u32[]{:S(2)}, u32[]{:S(2)}) collective-permute-start(bf16[192,1536]{1,0:T(8,128)(2,1)} %get-tuple-element.109.rest_1_), channel_id=1, source_target_pairs={{0,2},{1,3},{2,0},{3,1},{4,6},{5,7},{6,4},{7,5},{8,10},{9,11},{10,... | collective-permute-start | bytes 1769480 | tf_op jit(solution)/shard_map/ppermute | solution.py:736
  182.9 27.7 %collective-permute-start.20 = (bf16[48,3072]{1,0:T(8,128)(2,1)}, bf16[48,3072]{1,0:T(8,128)(2,1)S(1)}, u32[]{:S(2)}, u32[]{:S(2)}) collective-permute-start(bf16[48,3072]{1,0:T(8,128)(2,1)} %get-tuple-element.117.rest_0_), channel_id=1, source_target_pairs={{0,8},{4,12},{8,0},{12,4},{16,24},{20,28},{24,16},{28,20},{1,9},{5... | collective-permute-start | bytes 884744 | tf_op jit(solution)/shard_map/ppermute | solution.py:736
  184.5 26.1 %collective-permute-start.21 = (bf16[48,3072]{1,0:T(8,128)(2,1)}, bf16[48,3072]{1,0:T(8,128)(2,1)S(1)}, u32[]{:S(2)}, u32[]{:S(2)}) collective-permute-start(bf16[48,3072]{1,0:T(8,128)(2,1)} %get-tuple-element.118.rest_1_), channel_id=1, source_target_pairs={{0,16},{4,20},{8,24},{12,28},{16,0},{20,4},{24,8},{28,12},{1,17},{... | collective-permute-start | bytes 884744 | tf_op jit(solution)/shard_map/ppermute | solution.py:736
  187.1 23.5 %collective-permute-start.22 = (bf16[48,3072]{1,0:T(8,128)(2,1)}, bf16[48,3072]{1,0:T(8,128)(2,1)S(1)}, u32[]{:S(2)}, u32[]{:S(2)}) collective-permute-start(bf16[48,3072]{1,0:T(8,128)(2,1)} %get-tuple-element.119.rest_2_), channel_id=1, source_target_pairs={{0,24},{4,28},{8,16},{12,20},{16,8},{20,12},{24,0},{28,4},{1,25},{... | collective-permute-start | bytes 884744 | tf_op jit(solution)/shard_map/ppermute | solution.py:736
  215.0 25.2 %collective-permute-start.8 = (bf16[8,64,768]{2,1,0:T(8,128)(2,1)S(1)}, bf16[8,64,768]{2,1,0:T(8,128)(2,1)S(1)}, u32[]{:S(2)}, u32[]{:S(2)}) collective-permute-start(bf16[8,64,768]{2,1,0:T(8,128)(2,1)S(1)} %copy-done.42), channel_id=1, source_target_pairs={{0,1},{1,0},{2,3},{3,2},{4,5},{5,4},{6,7},{7,6},{8,9},{9,8},{10,11... | collective-permute-start | bytes 2359304 | tf_op jit(solution)/shard_map/ppermute | solution.py:736
  216.3 16.8 %collective-permute-start.18 = (bf16[384,384]{1,0:T(8,128)(2,1)}, bf16[384,384]{1,0:T(8,128)(2,1)S(1)}, u32[]{:S(2)}, u32[]{:S(2)}) collective-permute-start(bf16[384,384]{1,0:T(8,128)(2,1)} %get-tuple-element.121), channel_id=1, source_target_pairs={{0,2},{1,3},{2,0},{3,1},{4,6},{5,7},{6,4},{7,5},{8,10},{9,11},{10,... | collective-permute-start | bytes 884744 | tf_op jit(solution)/shard_map/ppermute | solution.py:736
  217.1 16.0 %collective-permute-start.19 = (bf16[384,384]{1,0:T(8,128)(2,1)}, bf16[384,384]{1,0:T(8,128)(2,1)S(1)}, u32[]{:S(2)}, u32[]{:S(2)}) collective-permute-start(bf16[384,384]{1,0:T(8,128)(2,1)} %get-tuple-element.124), channel_id=1, source_target_pairs={{0,4},{4,0},{8,12},{12,8},{16,20},{20,16},{24,28},{28,24},{1,5},{5... | collective-permute-start | bytes 884744 | tf_op jit(solution)/shard_map/ppermute | solution.py:736
  225.1 34.3 %collective-permute-start.24 = (bf16[8,64,768]{2,1,0:T(8,128)(2,1)}, bf16[8,64,768]{2,1,0:T(8,128)(2,1)S(1)}, u32[]{:S(2)}, u32[]{:S(2)}) collective-permute-start(bf16[8,64,768]{2,1,0:T(8,128)(2,1)} %get-tuple-element.132), channel_id=1, source_target_pairs={{0,1},{1,0},{2,3},{3,2},{4,5},{5,4},{6,7},{7,6},{8,9},{9,8},{10,11... | collective-permute-start | bytes 2359304 | tf_op jit(solution)/shard_map/ppermute | solution.py:736
  237.5 11.5 %collective-permute-start.25 = (bf16[192,768]{1,0:T(8,128)(2,1)}, bf16[192,768]{1,0:T(8,128)(2,1)S(1)}, u32[]{:S(2)}, u32[]{:S(2)}) collective-permute-start(bf16[192,768]{1,0:T(8,128)(2,1)} %get-tuple-element.128.rest_0_), channel_id=1, source_target_pairs={{0,4},{4,0},{8,12},{12,8},{16,20},{20,16},{24,28},{28,24},{1,5},{5... | collective-permute-start | bytes 884744 | tf_op jit(solution)/shard_map/ppermute | solution.py:736
  239.0 12.4 %collective-permute-start.26 = (bf16[192,768]{1,0:T(8,128)(2,1)}, bf16[192,768]{1,0:T(8,128)(2,1)S(1)}, u32[]{:S(2)}, u32[]{:S(2)}) collective-permute-start(bf16[192,768]{1,0:T(8,128)(2,1)} %get-tuple-element.129.rest_1_), channel_id=1, source_target_pairs={{0,2},{1,3},{2,0},{3,1},{4,6},{5,7},{6,4},{7,5},{8,10},{9,11},{10,... | collective-permute-start | bytes 884744 | tf_op jit(solution)/shard_map/ppermute | solution.py:736
  255.9 17.0 %collective-permute-start.32 = (bf16[48,1536]{1,0:T(8,128)(2,1)}, bf16[48,1536]{1,0:T(8,128)(2,1)S(1)}, u32[]{:S(2)}, u32[]{:S(2)}) collective-permute-start(bf16[48,1536]{1,0:T(8,128)(2,1)} %get-tuple-element.137.rest_1_), channel_id=1, source_target_pairs={{0,16},{4,20},{8,24},{12,28},{16,0},{20,4},{24,8},{28,12},{1,17},{... | collective-permute-start | bytes 442376 | tf_op jit(solution)/shard_map/ppermute | solution.py:736
  259.4 13.6 %collective-permute-start.33 = (bf16[48,1536]{1,0:T(8,128)(2,1)}, bf16[48,1536]{1,0:T(8,128)(2,1)S(1)}, u32[]{:S(2)}, u32[]{:S(2)}) collective-permute-start(bf16[48,1536]{1,0:T(8,128)(2,1)} %get-tuple-element.138.rest_2_), channel_id=1, source_target_pairs={{0,24},{4,28},{8,16},{12,20},{16,8},{20,12},{24,0},{28,4},{1,25},{... | collective-permute-start | bytes 442376 | tf_op jit(solution)/shard_map/ppermute | solution.py:736
  276.5 31.7 %collective-permute-start.36 = (bf16[48,1536]{1,0:T(8,128)(2,1)}, bf16[48,1536]{1,0:T(8,128)(2,1)S(1)}, u32[]{:S(2)}, u32[]{:S(2)}) collective-permute-start(bf16[48,1536]{1,0:T(8,128)(2,1)} %total.3), channel_id=1, source_target_pairs={{0,24},{4,28},{8,16},{12,20},{16,8},{20,12},{24,0},{28,4},{1,25},{... | collective-permute-start | bytes 442376 | tf_op jit(solution)/shard_map/ppermute | solution.py:736
  277.5 30.0 %collective-permute-start.35 = (bf16[48,1536]{1,0:T(8,128)(2,1)}, bf16[48,1536]{1,0:T(8,128)(2,1)S(1)}, u32[]{:S(2)}, u32[]{:S(2)}) collective-permute-start(bf16[48,1536]{1,0:T(8,128)(2,1)} %total.3), channel_id=1, source_target_pairs={{0,16},{4,20},{8,24},{12,28},{16,0},{20,4},{24,8},{28,12},{1,17},{... | collective-permute-start | bytes 442376 | tf_op jit(solution)/shard_map/ppermute | solution.py:736
  280.1 16.0 %collective-permute-start.34 = (bf16[48,1536]{1,0:T(8,128)(2,1)}, bf16[48,1536]{1,0:T(8,128)(2,1)S(1)}, u32[]{:S(2)}, u32[]{:S(2)}) collective-permute-start(bf16[48,1536]{1,0:T(8,128)(2,1)} %total.3), channel_id=1, source_target_pairs={{0,8},{4,12},{8,0},{12,4},{16,24},{20,28},{24,16},{28,20},{1,9},{5... | collective-permute-start | bytes 442376 | tf_op jit(solution)/shard_map/ppermute | solution.py:736
  310.6 13.5 %collective-permute-start.42 = (f32[9,2688]{1,0:T(8,128)S(1)}, f32[9,2688]{1,0:T(8,128)S(1)}, u32[]{:S(2)}, u32[]{:S(2)}) collective-permute-start(f32[9,2688]{1,0:T(8,128)S(1)} %constant_dynamic-update-slice_fusion.22), channel_id=1, source_target_pairs={{0,4},{4,0},{8,12},{12,8},{16,20},{20,16},{24,28},{28,24},{1,5},{5... | collective-permute-start | bytes 290312 | tf_op jit(solution)/shard_map/ppermute | solution.py:736
  316.7 27.5 %collective-permute-start.40 = (bf16[384,768]{1,0:T(8,128)(2,1)}, bf16[384,768]{1,0:T(8,128)(2,1)S(1)}, u32[]{:S(2)}, u32[]{:S(2)}) collective-permute-start(bf16[384,768]{1,0:T(8,128)(2,1)} %get-tuple-element.166), channel_id=1, source_target_pairs={{0,4},{4,0},{8,12},{12,8},{16,20},{20,16},{24,28},{28,24},{1,5},{5... | collective-permute-start | bytes 1769480 | tf_op jit(solution)/shard_map/ppermute | solution.py:736
  321.1 23.9 %collective-permute-start.38 = (bf16[384,768]{1,0:T(8,128)(2,1)}, bf16[384,768]{1,0:T(8,128)(2,1)S(1)}, u32[]{:S(2)}, u32[]{:S(2)}) collective-permute-start(bf16[384,768]{1,0:T(8,128)(2,1)} %get-tuple-element.164), channel_id=1, source_target_pairs={{0,2},{1,3},{2,0},{3,1},{4,6},{5,7},{6,4},{7,5},{8,10},{9,11},{10,... | collective-permute-start | bytes 1769480 | tf_op jit(solution)/shard_map/ppermute | solution.py:736
  339.2 16.8 %collective-permute-start.23 = (bf16[256,768]{1,0:T(8,128)(2,1)}, bf16[256,768]{1,0:T(8,128)(2,1)}, u32[]{:S(2)}, u32[]{:S(2)}) collective-permute-start(bf16[256,768]{1,0:T(8,128)(2,1)} %get-tuple-element.131), channel_id=1, source_target_pairs={{0,2},{1,3},{2,0},{3,1},{4,6},{5,7},{6,4},{7,5},{8,10},{9,11},{10,... | collective-permute-start | bytes 1179656 | tf_op jit(solution)/shard_map/ppermute | solution.py:736
  346.6 22.1 %collective-permute-start.41 = (bf16[768,1536]{1,0:T(8,128)(2,1)S(1)}, bf16[768,1536]{1,0:T(8,128)(2,1)}, u32[]{:S(2)}, u32[]{:S(2)}) collective-permute-start(bf16[768,1536]{1,0:T(8,128)(2,1)S(1)} %pad_maximum_fusion.one.two), channel_id=1, source_target_pairs={{0,1},{1,0},{2,3},{3,2},{4,5},{5,4},{6,7},{7,6},{8,9},{9,8},{10,11... | collective-permute-start | bytes 7077896 | tf_op jit(solution)/shard_map/ppermute | solution.py:736
  353.9 13.5 %collective-permute-start.27 = (bf16[256,768]{1,0:T(8,128)(2,1)}, bf16[256,768]{1,0:T(8,128)(2,1)S(1)}, u32[]{:S(2)}, u32[]{:S(2)}) collective-permute-start(bf16[256,768]{1,0:T(8,128)(2,1)} %get-tuple-element.140), channel_id=1, source_target_pairs={{0,2},{1,3},{2,0},{3,1},{4,6},{5,7},{6,4},{7,5},{8,10},{9,11},{10,... | collective-permute-start | bytes 1179656 | tf_op jit(solution)/shard_map/ppermute | solution.py:736
  354.6 11.6 %collective-permute-start.30 = (f32[6,768]{1,0:T(8,128)S(1)}, f32[6,768]{1,0:T(8,128)S(1)}, u32[]{:S(2)}, u32[]{:S(2)}) collective-permute-start(f32[6,768]{1,0:T(8,128)S(1)} %add.94), channel_id=1, source_target_pairs={{0,2},{1,3},{2,0},{3,1},{4,6},{5,7},{6,4},{7,5},{8,10},{9,11},{10,... | collective-permute-start | bytes 55304 | tf_op jit(solution)/shard_map/ppermute | solution.py:736
  (64 other events, 429.6 us)
Sparse Core Ops, SparseCore 0:
  214.5 101.9 all-gather.2
